TPU v7x, 128 devices: a whole 4x4x4 slice. The times are simulated.
128 devices in a mesh: grp: 8 (over x, core), tile: 16 (over y, z).
Axes of the slice: x: 4, y: 4, z: 4, core: 2. Of those that a mesh axis runs over, the one named last changes fastest.
Arguments:
- molecule_coords: float32 [3, 2097152], P(None, ('grp', 'tile')), may hold values from 0 to 1.6
- molecule_speeds: float32 [3, 2097152], P(None, ('grp', 'tile')), may hold values from -6 to 6
- molecule_thermal_state: float32 [2097152], P(('grp', 'tile')), may hold values from 0.5 to 2
- conservative_strength: float32 [2097152], P(('grp', 'tile')), may hold values from 0.05 to 0.5
- noise_keys: int32 [2097152], P(('grp', 'tile')), may hold values from 0 to 32767
- exported_tile_places: int32 [128, 16, 12], P(('grp', 'tile')), may hold values from 0 to 127
- tile_couplings: int32 [128, 1024, 2], P(('grp', 'tile')), may hold values from 0 to 383, as said below
- processor_coupling_tally: int32 [128], P(('grp', 'tile')), may hold values from 512 to 1024
Outputs:
- force_heat: float32 [4, 2097152], P(None, ('grp', 'tile'))
Inputs may be any that keep to these rules, and one draw needn't show every extreme that they name: `tile_couplings`: second slots of workers in the lowest slab are below 192; first slots are below 192.
All inputs are finite; a program needn't handle non-finite values.
Results may differ from a plain program's by a relative error of at most 0.0003.
Values sent between devices are 32-bit elements; how exact they have to be, the bound alone decides.
A program may use at most 128 MiB of HBM per device.

v0:
```python
import math
import jax
import jax.numpy as jnp
from jax import lax
from jax.sharding import PartitionSpec as P

friction = 0.45
noise_amp = 0.3
conductivity = 0.1


def passed_along(value, axis, steps):
    count = lax.axis_size(axis)
    leading, last = (max(0, -steps), min(count, count - steps))
    return lax.ppermute(value, axis, [(source, source + steps) for source in range(leading, last)])


def tile_pair(first, second):
    offset = first[0:3, :, None] - second[0:3, None, :]
    radius = jnp.sqrt(jnp.sum(offset * offset, 0) + 0.01)
    unit = offset / radius
    weight = jnp.maximum(1.0 - radius, 0.0)
    relative = first[3:6, :, None] - second[3:6, None, :]
    along = jnp.sum(unit * relative, 0)
    repulse = 0.5 * (first[7][:, None] + second[7][None, :])
    seed_first = first[8].astype(jnp.int32)
    seed_second = second[8].astype(jnp.int32)
    hashed = (
        seed_first[:, None] * seed_second[None, :] + seed_first[:, None] + seed_second[None, :]
    ) % 65521
    noise = hashed.astype(jnp.float32) * (2.0 / 65521.0) - 1.0
    magnitude = repulse * weight - friction * weight * weight * along + noise_amp * weight * noise
    force = magnitude[None] * unit
    conduct = conductivity * weight * weight * (second[6][None, :] - first[6][:, None])
    viscous = 0.5 * friction * weight * weight * along * along
    on_first = jnp.concatenate([jnp.sum(force, 2), jnp.sum(conduct + viscous, 1)[None]], 0)
    on_second = jnp.concatenate([-jnp.sum(force, 1), jnp.sum(viscous - conduct, 0)[None]], 0)
    return (on_first, on_second)


def tile_self(block_data):
    offset = block_data[0:3, :, None] - block_data[0:3, None, :]
    radius = jnp.sqrt(jnp.sum(offset * offset, 0) + 0.01)
    unit = offset / radius
    weight = jnp.maximum(1.0 - radius, 0.0)
    relative = block_data[3:6, :, None] - block_data[3:6, None, :]
    along = jnp.sum(unit * relative, 0)
    repulse = 0.5 * (block_data[7][:, None] + block_data[7][None, :])
    seed_first = block_data[8].astype(jnp.int32)
    hashed = (
        seed_first[:, None] * seed_first[None, :] + seed_first[:, None] + seed_first[None, :]
    ) % 65521
    noise = hashed.astype(jnp.float32) * (2.0 / 65521.0) - 1.0
    others = 1.0 - jnp.eye(block_data.shape[1], dtype=jnp.float32)
    magnitude = (
        repulse * weight - friction * weight * weight * along + noise_amp * weight * noise
    ) * others
    force = magnitude[None] * unit
    conduct = conductivity * weight * weight * (block_data[6][None, :] - block_data[6][:, None])
    viscous = 0.5 * friction * weight * weight * along * along
    heating = jnp.sum((conduct + viscous) * others, 1)
    return jnp.concatenate([jnp.sum(force, 2), heating[None]], 0)


def one_hot(indices, count):
    return (indices[:, None] == jnp.arange(count, dtype=jnp.int32)[None, :]).astype(jnp.float32)


def per_device(
    molecule_coords,
    molecule_speeds,
    molecule_thermal_state,
    conservative_strength,
    noise_keys,
    exported_tile_places,
    tile_couplings,
    processor_coupling_tally,
):
    n_tile = lax.axis_size("tile")
    blocks = molecule_coords.shape[1] // 128
    slot_table = exported_tile_places[0]
    cap = slot_table.shape[1]
    buffer_len = n_tile * cap
    owned = jnp.concatenate(
        [
            molecule_coords,
            molecule_speeds,
            molecule_thermal_state[None],
            conservative_strength[None],
            noise_keys[None].astype(jnp.float32),
        ],
        0,
    )
    owned = owned.reshape(9, blocks, 128).transpose(1, 0, 2)
    group_data = lax.all_gather(owned, "tile", axis=0, tiled=True)
    tables = lax.all_gather(exported_tile_places, "tile", axis=0, tiled=True)
    my_index = lax.axis_index("tile")
    my_slots = lax.dynamic_index_in_dim(tables, my_index, 1, keepdims=False)
    group_ids = (jnp.arange(n_tile, dtype=jnp.int32)[:, None] * blocks + my_slots).reshape(-1)
    held_blocks = group_data[group_ids]
    neighbour = passed_along(held_blocks, "grp", 1)
    reachable = jnp.concatenate([held_blocks, neighbour], 0)
    total_pair_count = tile_couplings.shape[1]
    batch = math.gcd(total_pair_count, 64)
    first_slots = tile_couplings[0, :, 0].reshape(-1, batch)
    second_slots = tile_couplings[0, :, 1].reshape(-1, batch)
    live_rows = (
        (jnp.arange(total_pair_count, dtype=jnp.int32) < processor_coupling_tally[0])
        .astype(jnp.float32)
        .reshape(-1, batch)
    )

    def consume(carry, items):
        near_acc, far_acc = carry
        first_idx, second_index, live = items
        on_first, on_second = jax.vmap(tile_pair)(held_blocks[first_idx], reachable[second_index])
        on_first = (on_first * live[:, None, None]).reshape(batch, 512)
        on_second = (on_second * live[:, None, None]).reshape(batch, 512)
        near_acc = near_acc + jnp.dot(
            one_hot(first_idx, buffer_len).T, on_first, precision=lax.Precision.HIGHEST
        )
        far_acc = far_acc + jnp.dot(
            one_hot(second_index, 2 * buffer_len).T, on_second, precision=lax.Precision.HIGHEST
        )
        return ((near_acc, far_acc), None)

    start_carry = (
        jnp.zeros((buffer_len, 512), jnp.float32),
        jnp.zeros((2 * buffer_len, 512), jnp.float32),
    )
    (near_acc, far_acc), _ = lax.scan(consume, start_carry, (first_slots, second_slots, live_rows))
    lower_terms = passed_along(far_acc[buffer_len:], "grp", -1)
    own_total = near_acc + far_acc[:buffer_len] + lower_terms
    selector = one_hot(group_ids, n_tile * blocks)
    summed = lax.psum_scatter(
        jnp.dot(selector.T, own_total, precision=lax.Precision.HIGHEST),
        "tile",
        scatter_dimension=0,
        tiled=True,
    )
    self_batch = math.gcd(blocks, 16)

    def self_step(carry, group_data):
        return (carry, jax.vmap(tile_self)(group_data))

    _, selfs = lax.scan(
        self_step, jnp.zeros((), jnp.float32), owned.reshape(-1, self_batch, 9, 128)
    )
    result = summed.reshape(blocks, 4, 128) + selfs.reshape(blocks, 4, 128)
    return result.transpose(1, 0, 2).reshape(4, blocks * 128)


def solution(mesh):
    in_specs = (
        P(None, ("grp", "tile")),
        P(None, ("grp", "tile")),
        P(("grp", "tile")),
        P(("grp", "tile")),
        P(("grp", "tile")),
        P(("grp", "tile"), None, None),
        P(("grp", "tile"), None, None),
        P(("grp", "tile")),
    )
    out_specs = P(None, ("grp", "tile"))
    return jax.shard_map(
        per_device, mesh=mesh, in_specs=in_specs, out_specs=out_specs, check_vma=False
    )
```

profile of v0, /device:TPU:0, one launch (start us, length us, event | category | flops | bytes accessed | tf_op | source)
XLA Modules:
  0.0 833.5 jit_solution(1761941762387604038)
XLA Ops:
  12.7 25.4 %all_gather.6 = s32[16,16,12]{2,1,0:T(8,128)S(1)} all-gather(s32[1,16,12]{2,1,0:T(8,128)S(1)} %copy.32), channel_id=1, replica_groups=mesh['grp'=8,'tile'=16] {'tile'}, dimensions={0}, use_global_device_ids=true | all-gather | bytes 13056 | tf_op jit(solution)/shard_map/all_gather | solution.py:96
  40.1 50.3 %all-gather.2.cloned.1.call-done = f32[2048,9,128]{2,0,1:T(8,128)} async-done(((f32[128,9,128]{2,0,1:T(8,128)}), f32[2048,9,128]{2,0,1:T(8,128)}) %all-gather.2.cloned.1.call-update) | async-done | bytes 9437200 | tf_op jit(solution)/shard_map/all_gather | solution.py:95
  90.5 12.8 %copy.33 = f32[2048,9,128]{2,1,0:T(8,128)} copy(f32[2048,9,128]{2,0,1:T(8,128)} %all-gather.2.cloned.1.call-done) | data formatting | bytes 18874368 | tf_op jit(solution)/shard_map/all_gather | solution.py:95
  117.3 606.1 %while.28 = (s32[]{:T(128)}, f32[192,512]{1,0:T(8,128)}, f32[384,512]{1,0:T(8,128)S(1)}, s32[16,64]{1,0:T(8,128)S(1)}, f32[192,9,128]{2,1,0:T(8,128)S(1)}, /*ind...) while((s32[]{:T(128)}, f32[192,512]{1,0:T(8,128)}, ...), condition=%wide.region_7.8_spmd.clone, body=%wide.region_0.7_spmd.clone.sunk | while | flops 305871232 | bytes 52507452 | solution.py:131
  126.5 8.0 multiply_reduce_fusion.11
  134.7 9.2 %subtract_reduce_fusion.2 = (f32[64,128]{1,0:T(8,128)S(1)}, f32[64,128]{1,0:T(8,128)S(1)}, f32[64,128,128]{2,1,0:T(8,128)S(1)}) fusion(f32[64,128,128]{2,1,0:T(8,128)S(1)} %multiply_reduce_fusion.11, f32[64,128]{1,0:T(8,128)S(1)} %bitcast.118, f32[64,128]{1,0:T(8,128)S(1)} %bitcast.115, f32[64,128,128]{2,1,0:T(8,128)S(1)} %fusion.72, ...), kind=kLoop, calls=%fused_computation.59.clone.1 | loop fusion | flops 38780928 | bytes 12845056 | tf_op jit(solution)/shard_map/while/body/eval_jaxpr/vmap()/reduce_sum | solution.py:37
  143.9 8.5 %multiply_reduce_fusion.12 = (f32[64,3,128]{2,1,0:T(4,128)S(1)}, f32[64,3,128]{2,1,0:T(4,128)S(1)}) fusion(f32[64,128,128]{2,1,0:T(8,128)S(1)} %get-tuple-element.365, f32[64,128,128]{2,1,0:T(8,128)S(1)} %add_sqrt_fusion.5, f32[64,3,128]{2,1,0:T(4,128)S(1)} %get-tuple-element.356, f32[64,3,128]{2,1,0:T(4,128)S(1)} %get-tuple-element.357), kind=kLoop, calls=%fused_computation.44.clone.1 | loop fusion | flops 15679488 | bytes 8781824 | tf_op jit(solution)/shard_map/while/body/eval_jaxpr/vmap()/reduce_sum | solution.py:37
  172.6 9.2 %subtract_reduce_fusion.2 = (f32[64,128]{1,0:T(8,128)S(1)}, f32[64,128]{1,0:T(8,128)S(1)}, f32[64,128,128]{2,1,0:T(8,128)S(1)}) fusion(f32[64,128,128]{2,1,0:T(8,128)S(1)} %multiply_reduce_fusion.11, f32[64,128]{1,0:T(8,128)S(1)} %bitcast.118, f32[64,128]{1,0:T(8,128)S(1)} %bitcast.115, f32[64,128,128]{2,1,0:T(8,128)S(1)} %fusion.72, ...), kind=kLoop, calls=%fused_computation.59.clone.1 | loop fusion | flops 38780928 | bytes 12845056 | tf_op jit(solution)/shard_map/while/body/eval_jaxpr/vmap()/reduce_sum | solution.py:37
  181.8 8.5 %multiply_reduce_fusion.12 = (f32[64,3,128]{2,1,0:T(4,128)S(1)}, f32[64,3,128]{2,1,0:T(4,128)S(1)}) fusion(f32[64,128,128]{2,1,0:T(8,128)S(1)} %get-tuple-element.365, f32[64,128,128]{2,1,0:T(8,128)S(1)} %add_sqrt_fusion.5, f32[64,3,128]{2,1,0:T(4,128)S(1)} %get-tuple-element.356, f32[64,3,128]{2,1,0:T(4,128)S(1)} %get-tuple-element.357), kind=kLoop, calls=%fused_computation.44.clone.1 | loop fusion | flops 15679488 | bytes 8781824 | tf_op jit(solution)/shard_map/while/body/eval_jaxpr/vmap()/reduce_sum | solution.py:37
  202.3 8.0 multiply_reduce_fusion.11
  210.4 9.2 %subtract_reduce_fusion.2 = (f32[64,128]{1,0:T(8,128)S(1)}, f32[64,128]{1,0:T(8,128)S(1)}, f32[64,128,128]{2,1,0:T(8,128)S(1)}) fusion(f32[64,128,128]{2,1,0:T(8,128)S(1)} %multiply_reduce_fusion.11, f32[64,128]{1,0:T(8,128)S(1)} %bitcast.118, f32[64,128]{1,0:T(8,128)S(1)} %bitcast.115, f32[64,128,128]{2,1,0:T(8,128)S(1)} %fusion.72, ...), kind=kLoop, calls=%fused_computation.59.clone.1 | loop fusion | flops 38780928 | bytes 12845056 | tf_op jit(solution)/shard_map/while/body/eval_jaxpr/vmap()/reduce_sum | solution.py:37
  219.7 8.5 %multiply_reduce_fusion.12 = (f32[64,3,128]{2,1,0:T(4,128)S(1)}, f32[64,3,128]{2,1,0:T(4,128)S(1)}) fusion(f32[64,128,128]{2,1,0:T(8,128)S(1)} %get-tuple-element.365, f32[64,128,128]{2,1,0:T(8,128)S(1)} %add_sqrt_fusion.5, f32[64,3,128]{2,1,0:T(4,128)S(1)} %get-tuple-element.356, f32[64,3,128]{2,1,0:T(4,128)S(1)} %get-tuple-element.357), kind=kLoop, calls=%fused_computation.44.clone.1 | loop fusion | flops 15679488 | bytes 8781824 | tf_op jit(solution)/shard_map/while/body/eval_jaxpr/vmap()/reduce_sum | solution.py:37
  240.2 8.0 multiply_reduce_fusion.11
  248.3 9.2 %subtract_reduce_fusion.2 = (f32[64,128]{1,0:T(8,128)S(1)}, f32[64,128]{1,0:T(8,128)S(1)}, f32[64,128,128]{2,1,0:T(8,128)S(1)}) fusion(f32[64,128,128]{2,1,0:T(8,128)S(1)} %multiply_reduce_fusion.11, f32[64,128]{1,0:T(8,128)S(1)} %bitcast.118, f32[64,128]{1,0:T(8,128)S(1)} %bitcast.115, f32[64,128,128]{2,1,0:T(8,128)S(1)} %fusion.72, ...), kind=kLoop, calls=%fused_computation.59.clone.1 | loop fusion | flops 38780928 | bytes 12845056 | tf_op jit(solution)/shard_map/while/body/eval_jaxpr/vmap()/reduce_sum | solution.py:37
  257.5 8.5 %multiply_reduce_fusion.12 = (f32[64,3,128]{2,1,0:T(4,128)S(1)}, f32[64,3,128]{2,1,0:T(4,128)S(1)}) fusion(f32[64,128,128]{2,1,0:T(8,128)S(1)} %get-tuple-element.365, f32[64,128,128]{2,1,0:T(8,128)S(1)} %add_sqrt_fusion.5, f32[64,3,128]{2,1,0:T(4,128)S(1)} %get-tuple-element.356, f32[64,3,128]{2,1,0:T(4,128)S(1)} %get-tuple-element.357), kind=kLoop, calls=%fused_computation.44.clone.1 | loop fusion | flops 15679488 | bytes 8781824 | tf_op jit(solution)/shard_map/while/body/eval_jaxpr/vmap()/reduce_sum | solution.py:37
  278.0 8.0 multiply_reduce_fusion.11
  286.2 9.2 %subtract_reduce_fusion.2 = (f32[64,128]{1,0:T(8,128)S(1)}, f32[64,128]{1,0:T(8,128)S(1)}, f32[64,128,128]{2,1,0:T(8,128)S(1)}) fusion(f32[64,128,128]{2,1,0:T(8,128)S(1)} %multiply_reduce_fusion.11, f32[64,128]{1,0:T(8,128)S(1)} %bitcast.118, f32[64,128]{1,0:T(8,128)S(1)} %bitcast.115, f32[64,128,128]{2,1,0:T(8,128)S(1)} %fusion.72, ...), kind=kLoop, calls=%fused_computation.59.clone.1 | loop fusion | flops 38780928 | bytes 12845056 | tf_op jit(solution)/shard_map/while/body/eval_jaxpr/vmap()/reduce_sum | solution.py:37
  295.4 8.5 %multiply_reduce_fusion.12 = (f32[64,3,128]{2,1,0:T(4,128)S(1)}, f32[64,3,128]{2,1,0:T(4,128)S(1)}) fusion(f32[64,128,128]{2,1,0:T(8,128)S(1)} %get-tuple-element.365, f32[64,128,128]{2,1,0:T(8,128)S(1)} %add_sqrt_fusion.5, f32[64,3,128]{2,1,0:T(4,128)S(1)} %get-tuple-element.356, f32[64,3,128]{2,1,0:T(4,128)S(1)} %get-tuple-element.357), kind=kLoop, calls=%fused_computation.44.clone.1 | loop fusion | flops 15679488 | bytes 8781824 | tf_op jit(solution)/shard_map/while/body/eval_jaxpr/vmap()/reduce_sum | solution.py:37
  315.9 8.0 multiply_reduce_fusion.11
  324.1 9.2 %subtract_reduce_fusion.2 = (f32[64,128]{1,0:T(8,128)S(1)}, f32[64,128]{1,0:T(8,128)S(1)}, f32[64,128,128]{2,1,0:T(8,128)S(1)}) fusion(f32[64,128,128]{2,1,0:T(8,128)S(1)} %multiply_reduce_fusion.11, f32[64,128]{1,0:T(8,128)S(1)} %bitcast.118, f32[64,128]{1,0:T(8,128)S(1)} %bitcast.115, f32[64,128,128]{2,1,0:T(8,128)S(1)} %fusion.72, ...), kind=kLoop, calls=%fused_computation.59.clone.1 | loop fusion | flops 38780928 | bytes 12845056 | tf_op jit(solution)/shard_map/while/body/eval_jaxpr/vmap()/reduce_sum | solution.py:37
  333.3 8.5 %multiply_reduce_fusion.12 = (f32[64,3,128]{2,1,0:T(4,128)S(1)}, f32[64,3,128]{2,1,0:T(4,128)S(1)}) fusion(f32[64,128,128]{2,1,0:T(8,128)S(1)} %get-tuple-element.365, f32[64,128,128]{2,1,0:T(8,128)S(1)} %add_sqrt_fusion.5, f32[64,3,128]{2,1,0:T(4,128)S(1)} %get-tuple-element.356, f32[64,3,128]{2,1,0:T(4,128)S(1)} %get-tuple-element.357), kind=kLoop, calls=%fused_computation.44.clone.1 | loop fusion | flops 15679488 | bytes 8781824 | tf_op jit(solution)/shard_map/while/body/eval_jaxpr/vmap()/reduce_sum | solution.py:37
  353.8 8.0 multiply_reduce_fusion.11
  362.0 9.2 %subtract_reduce_fusion.2 = (f32[64,128]{1,0:T(8,128)S(1)}, f32[64,128]{1,0:T(8,128)S(1)}, f32[64,128,128]{2,1,0:T(8,128)S(1)}) fusion(f32[64,128,128]{2,1,0:T(8,128)S(1)} %multiply_reduce_fusion.11, f32[64,128]{1,0:T(8,128)S(1)} %bitcast.118, f32[64,128]{1,0:T(8,128)S(1)} %bitcast.115, f32[64,128,128]{2,1,0:T(8,128)S(1)} %fusion.72, ...), kind=kLoop, calls=%fused_computation.59.clone.1 | loop fusion | flops 38780928 | bytes 12845056 | tf_op jit(solution)/shard_map/while/body/eval_jaxpr/vmap()/reduce_sum | solution.py:37
  371.2 8.5 %multiply_reduce_fusion.12 = (f32[64,3,128]{2,1,0:T(4,128)S(1)}, f32[64,3,128]{2,1,0:T(4,128)S(1)}) fusion(f32[64,128,128]{2,1,0:T(8,128)S(1)} %get-tuple-element.365, f32[64,128,128]{2,1,0:T(8,128)S(1)} %add_sqrt_fusion.5, f32[64,3,128]{2,1,0:T(4,128)S(1)} %get-tuple-element.356, f32[64,3,128]{2,1,0:T(4,128)S(1)} %get-tuple-element.357), kind=kLoop, calls=%fused_computation.44.clone.1 | loop fusion | flops 15679488 | bytes 8781824 | tf_op jit(solution)/shard_map/while/body/eval_jaxpr/vmap()/reduce_sum | solution.py:37
  391.7 8.0 multiply_reduce_fusion.11
  399.9 9.2 %subtract_reduce_fusion.2 = (f32[64,128]{1,0:T(8,128)S(1)}, f32[64,128]{1,0:T(8,128)S(1)}, f32[64,128,128]{2,1,0:T(8,128)S(1)}) fusion(f32[64,128,128]{2,1,0:T(8,128)S(1)} %multiply_reduce_fusion.11, f32[64,128]{1,0:T(8,128)S(1)} %bitcast.118, f32[64,128]{1,0:T(8,128)S(1)} %bitcast.115, f32[64,128,128]{2,1,0:T(8,128)S(1)} %fusion.72, ...), kind=kLoop, calls=%fused_computation.59.clone.1 | loop fusion | flops 38780928 | bytes 12845056 | tf_op jit(solution)/shard_map/while/body/eval_jaxpr/vmap()/reduce_sum | solution.py:37
  409.1 8.5 %multiply_reduce_fusion.12 = (f32[64,3,128]{2,1,0:T(4,128)S(1)}, f32[64,3,128]{2,1,0:T(4,128)S(1)}) fusion(f32[64,128,128]{2,1,0:T(8,128)S(1)} %get-tuple-element.365, f32[64,128,128]{2,1,0:T(8,128)S(1)} %add_sqrt_fusion.5, f32[64,3,128]{2,1,0:T(4,128)S(1)} %get-tuple-element.356, f32[64,3,128]{2,1,0:T(4,128)S(1)} %get-tuple-element.357), kind=kLoop, calls=%fused_computation.44.clone.1 | loop fusion | flops 15679488 | bytes 8781824 | tf_op jit(solution)/shard_map/while/body/eval_jaxpr/vmap()/reduce_sum | solution.py:37
  437.7 9.2 %subtract_reduce_fusion.2 = (f32[64,128]{1,0:T(8,128)S(1)}, f32[64,128]{1,0:T(8,128)S(1)}, f32[64,128,128]{2,1,0:T(8,128)S(1)}) fusion(f32[64,128,128]{2,1,0:T(8,128)S(1)} %multiply_reduce_fusion.11, f32[64,128]{1,0:T(8,128)S(1)} %bitcast.118, f32[64,128]{1,0:T(8,128)S(1)} %bitcast.115, f32[64,128,128]{2,1,0:T(8,128)S(1)} %fusion.72, ...), kind=kLoop, calls=%fused_computation.59.clone.1 | loop fusion | flops 38780928 | bytes 12845056 | tf_op jit(solution)/shard_map/while/body/eval_jaxpr/vmap()/reduce_sum | solution.py:37
  446.9 8.5 %multiply_reduce_fusion.12 = (f32[64,3,128]{2,1,0:T(4,128)S(1)}, f32[64,3,128]{2,1,0:T(4,128)S(1)}) fusion(f32[64,128,128]{2,1,0:T(8,128)S(1)} %get-tuple-element.365, f32[64,128,128]{2,1,0:T(8,128)S(1)} %add_sqrt_fusion.5, f32[64,3,128]{2,1,0:T(4,128)S(1)} %get-tuple-element.356, f32[64,3,128]{2,1,0:T(4,128)S(1)} %get-tuple-element.357), kind=kLoop, calls=%fused_computation.44.clone.1 | loop fusion | flops 15679488 | bytes 8781824 | tf_op jit(solution)/shard_map/while/body/eval_jaxpr/vmap()/reduce_sum | solution.py:37
  467.4 8.0 multiply_reduce_fusion.11
  475.6 9.2 %subtract_reduce_fusion.2 = (f32[64,128]{1,0:T(8,128)S(1)}, f32[64,128]{1,0:T(8,128)S(1)}, f32[64,128,128]{2,1,0:T(8,128)S(1)}) fusion(f32[64,128,128]{2,1,0:T(8,128)S(1)} %multiply_reduce_fusion.11, f32[64,128]{1,0:T(8,128)S(1)} %bitcast.118, f32[64,128]{1,0:T(8,128)S(1)} %bitcast.115, f32[64,128,128]{2,1,0:T(8,128)S(1)} %fusion.72, ...), kind=kLoop, calls=%fused_computation.59.clone.1 | loop fusion | flops 38780928 | bytes 12845056 | tf_op jit(solution)/shard_map/while/body/eval_jaxpr/vmap()/reduce_sum | solution.py:37
  484.8 8.5 %multiply_reduce_fusion.12 = (f32[64,3,128]{2,1,0:T(4,128)S(1)}, f32[64,3,128]{2,1,0:T(4,128)S(1)}) fusion(f32[64,128,128]{2,1,0:T(8,128)S(1)} %get-tuple-element.365, f32[64,128,128]{2,1,0:T(8,128)S(1)} %add_sqrt_fusion.5, f32[64,3,128]{2,1,0:T(4,128)S(1)} %get-tuple-element.356, f32[64,3,128]{2,1,0:T(4,128)S(1)} %get-tuple-element.357), kind=kLoop, calls=%fused_computation.44.clone.1 | loop fusion | flops 15679488 | bytes 8781824 | tf_op jit(solution)/shard_map/while/body/eval_jaxpr/vmap()/reduce_sum | solution.py:37
  505.3 8.0 multiply_reduce_fusion.11
  513.5 9.2 %subtract_reduce_fusion.2 = (f32[64,128]{1,0:T(8,128)S(1)}, f32[64,128]{1,0:T(8,128)S(1)}, f32[64,128,128]{2,1,0:T(8,128)S(1)}) fusion(f32[64,128,128]{2,1,0:T(8,128)S(1)} %multiply_reduce_fusion.11, f32[64,128]{1,0:T(8,128)S(1)} %bitcast.118, f32[64,128]{1,0:T(8,128)S(1)} %bitcast.115, f32[64,128,128]{2,1,0:T(8,128)S(1)} %fusion.72, ...), kind=kLoop, calls=%fused_computation.59.clone.1 | loop fusion | flops 38780928 | bytes 12845056 | tf_op jit(solution)/shard_map/while/body/eval_jaxpr/vmap()/reduce_sum | solution.py:37
  522.7 8.5 %multiply_reduce_fusion.12 = (f32[64,3,128]{2,1,0:T(4,128)S(1)}, f32[64,3,128]{2,1,0:T(4,128)S(1)}) fusion(f32[64,128,128]{2,1,0:T(8,128)S(1)} %get-tuple-element.365, f32[64,128,128]{2,1,0:T(8,128)S(1)} %add_sqrt_fusion.5, f32[64,3,128]{2,1,0:T(4,128)S(1)} %get-tuple-element.356, f32[64,3,128]{2,1,0:T(4,128)S(1)} %get-tuple-element.357), kind=kLoop, calls=%fused_computation.44.clone.1 | loop fusion | flops 15679488 | bytes 8781824 | tf_op jit(solution)/shard_map/while/body/eval_jaxpr/vmap()/reduce_sum | solution.py:37
  551.4 9.2 %subtract_reduce_fusion.2 = (f32[64,128]{1,0:T(8,128)S(1)}, f32[64,128]{1,0:T(8,128)S(1)}, f32[64,128,128]{2,1,0:T(8,128)S(1)}) fusion(f32[64,128,128]{2,1,0:T(8,128)S(1)} %multiply_reduce_fusion.11, f32[64,128]{1,0:T(8,128)S(1)} %bitcast.118, f32[64,128]{1,0:T(8,128)S(1)} %bitcast.115, f32[64,128,128]{2,1,0:T(8,128)S(1)} %fusion.72, ...), kind=kLoop, calls=%fused_computation.59.clone.1 | loop fusion | flops 38780928 | bytes 12845056 | tf_op jit(solution)/shard_map/while/body/eval_jaxpr/vmap()/reduce_sum | solution.py:37
  560.6 8.5 %multiply_reduce_fusion.12 = (f32[64,3,128]{2,1,0:T(4,128)S(1)}, f32[64,3,128]{2,1,0:T(4,128)S(1)}) fusion(f32[64,128,128]{2,1,0:T(8,128)S(1)} %get-tuple-element.365, f32[64,128,128]{2,1,0:T(8,128)S(1)} %add_sqrt_fusion.5, f32[64,3,128]{2,1,0:T(4,128)S(1)} %get-tuple-element.356, f32[64,3,128]{2,1,0:T(4,128)S(1)} %get-tuple-element.357), kind=kLoop, calls=%fused_computation.44.clone.1 | loop fusion | flops 15679488 | bytes 8781824 | tf_op jit(solution)/shard_map/while/body/eval_jaxpr/vmap()/reduce_sum | solution.py:37
  589.2 9.2 %subtract_reduce_fusion.2 = (f32[64,128]{1,0:T(8,128)S(1)}, f32[64,128]{1,0:T(8,128)S(1)}, f32[64,128,128]{2,1,0:T(8,128)S(1)}) fusion(f32[64,128,128]{2,1,0:T(8,128)S(1)} %multiply_reduce_fusion.11, f32[64,128]{1,0:T(8,128)S(1)} %bitcast.118, f32[64,128]{1,0:T(8,128)S(1)} %bitcast.115, f32[64,128,128]{2,1,0:T(8,128)S(1)} %fusion.72, ...), kind=kLoop, calls=%fused_computation.59.clone.1 | loop fusion | flops 38780928 | bytes 12845056 | tf_op jit(solution)/shard_map/while/body/eval_jaxpr/vmap()/reduce_sum | solution.py:37
  598.4 8.5 %multiply_reduce_fusion.12 = (f32[64,3,128]{2,1,0:T(4,128)S(1)}, f32[64,3,128]{2,1,0:T(4,128)S(1)}) fusion(f32[64,128,128]{2,1,0:T(8,128)S(1)} %get-tuple-element.365, f32[64,128,128]{2,1,0:T(8,128)S(1)} %add_sqrt_fusion.5, f32[64,3,128]{2,1,0:T(4,128)S(1)} %get-tuple-element.356, f32[64,3,128]{2,1,0:T(4,128)S(1)} %get-tuple-element.357), kind=kLoop, calls=%fused_computation.44.clone.1 | loop fusion | flops 15679488 | bytes 8781824 | tf_op jit(solution)/shard_map/while/body/eval_jaxpr/vmap()/reduce_sum | solution.py:37
  627.1 9.2 %subtract_reduce_fusion.2 = (f32[64,128]{1,0:T(8,128)S(1)}, f32[64,128]{1,0:T(8,128)S(1)}, f32[64,128,128]{2,1,0:T(8,128)S(1)}) fusion(f32[64,128,128]{2,1,0:T(8,128)S(1)} %multiply_reduce_fusion.11, f32[64,128]{1,0:T(8,128)S(1)} %bitcast.118, f32[64,128]{1,0:T(8,128)S(1)} %bitcast.115, f32[64,128,128]{2,1,0:T(8,128)S(1)} %fusion.72, ...), kind=kLoop, calls=%fused_computation.59.clone.1 | loop fusion | flops 38780928 | bytes 12845056 | tf_op jit(solution)/shard_map/while/body/eval_jaxpr/vmap()/reduce_sum | solution.py:37
  636.3 8.5 %multiply_reduce_fusion.12 = (f32[64,3,128]{2,1,0:T(4,128)S(1)}, f32[64,3,128]{2,1,0:T(4,128)S(1)}) fusion(f32[64,128,128]{2,1,0:T(8,128)S(1)} %get-tuple-element.365, f32[64,128,128]{2,1,0:T(8,128)S(1)} %add_sqrt_fusion.5, f32[64,3,128]{2,1,0:T(4,128)S(1)} %get-tuple-element.356, f32[64,3,128]{2,1,0:T(4,128)S(1)} %get-tuple-element.357), kind=kLoop, calls=%fused_computation.44.clone.1 | loop fusion | flops 15679488 | bytes 8781824 | tf_op jit(solution)/shard_map/while/body/eval_jaxpr/vmap()/reduce_sum | solution.py:37
  665.0 9.2 %subtract_reduce_fusion.2 = (f32[64,128]{1,0:T(8,128)S(1)}, f32[64,128]{1,0:T(8,128)S(1)}, f32[64,128,128]{2,1,0:T(8,128)S(1)}) fusion(f32[64,128,128]{2,1,0:T(8,128)S(1)} %multiply_reduce_fusion.11, f32[64,128]{1,0:T(8,128)S(1)} %bitcast.118, f32[64,128]{1,0:T(8,128)S(1)} %bitcast.115, f32[64,128,128]{2,1,0:T(8,128)S(1)} %fusion.72, ...), kind=kLoop, calls=%fused_computation.59.clone.1 | loop fusion | flops 38780928 | bytes 12845056 | tf_op jit(solution)/shard_map/while/body/eval_jaxpr/vmap()/reduce_sum | solution.py:37
  674.2 8.5 %multiply_reduce_fusion.12 = (f32[64,3,128]{2,1,0:T(4,128)S(1)}, f32[64,3,128]{2,1,0:T(4,128)S(1)}) fusion(f32[64,128,128]{2,1,0:T(8,128)S(1)} %get-tuple-element.365, f32[64,128,128]{2,1,0:T(8,128)S(1)} %add_sqrt_fusion.5, f32[64,3,128]{2,1,0:T(4,128)S(1)} %get-tuple-element.356, f32[64,3,128]{2,1,0:T(4,128)S(1)} %get-tuple-element.357), kind=kLoop, calls=%fused_computation.44.clone.1 | loop fusion | flops 15679488 | bytes 8781824 | tf_op jit(solution)/shard_map/while/body/eval_jaxpr/vmap()/reduce_sum | solution.py:37
  702.9 9.2 %subtract_reduce_fusion.2 = (f32[64,128]{1,0:T(8,128)S(1)}, f32[64,128]{1,0:T(8,128)S(1)}, f32[64,128,128]{2,1,0:T(8,128)S(1)}) fusion(f32[64,128,128]{2,1,0:T(8,128)S(1)} %multiply_reduce_fusion.11, f32[64,128]{1,0:T(8,128)S(1)} %bitcast.118, f32[64,128]{1,0:T(8,128)S(1)} %bitcast.115, f32[64,128,128]{2,1,0:T(8,128)S(1)} %fusion.72, ...), kind=kLoop, calls=%fused_computation.59.clone.1 | loop fusion | flops 38780928 | bytes 12845056 | tf_op jit(solution)/shard_map/while/body/eval_jaxpr/vmap()/reduce_sum | solution.py:37
  712.1 8.5 %multiply_reduce_fusion.12 = (f32[64,3,128]{2,1,0:T(4,128)S(1)}, f32[64,3,128]{2,1,0:T(4,128)S(1)}) fusion(f32[64,128,128]{2,1,0:T(8,128)S(1)} %get-tuple-element.365, f32[64,128,128]{2,1,0:T(8,128)S(1)} %add_sqrt_fusion.5, f32[64,3,128]{2,1,0:T(4,128)S(1)} %get-tuple-element.356, f32[64,3,128]{2,1,0:T(4,128)S(1)} %get-tuple-element.357), kind=kLoop, calls=%fused_computation.44.clone.1 | loop fusion | flops 15679488 | bytes 8781824 | tf_op jit(solution)/shard_map/while/body/eval_jaxpr/vmap()/reduce_sum | solution.py:37
  725.8 10.5 %collective-permute-done.1 = f32[192,512]{1,0:T(8,128)S(1)} collective-permute-done((f32[192,512]{1,0:T(8,128)S(1)}, f32[192,512]{1,0:T(8,128)S(1)}, u32[]{:S(2)}, u32[]{:S(2)}) %collective-permute-start.1) | collective-permute-done | bytes 393248 | tf_op jit(solution)/shard_map/ppermute | solution.py:15
  741.3 69.2 %while.27 = (s32[]{:T(128)}, f32[8,16,4,128]{3,2,1,0:T(4,128)S(1)}, f32[8,16,9,128]{3,1,0,2:T(8,128)}, s32[]{:T(128)}) while((s32[]{:T(128)}, f32[8,16,4,128]{3,2,1,0:T(4,128)S(1)}, f32[8,16,9,128]{3,1,0,2:T(8,128)}, s32[]{:T(128)}) %tuple.104), condition=%wide.region_14.15_spmd, body=%wide.region_9.14_spmd.sunk | while | flops 18925568 | bytes 11239485 | solution.py:146
  810.5 14.3 %reduce-scatter.2.cloned.1.call-done = f32[128,512]{1,0:T(8,128)} async-done(((f32[2048,512]{1,0:T(8,128)}), f32[128,512]{1,0:T(8,128)}) %reduce-scatter.2.cloned.1.call-update) | async-done | bytes 262160 | tf_op jit(solution)/shard_map/reduce_scatter | solution.py:135
  (658 shorter events, 347.6 us)
Async XLA Ops:
  6.5 83.9 %all-gather.2.cloned.1.call-start = ((), (), s32[]{:S(2)}) async-start(), calls=%async_computation.1 | async-start | bytes 10027008 | tf_op jit(solution)/shard_map/all_gather | solution.py:95
  11.8 813.0 %reduce-scatter.2.cloned.1.call-start = ((), (), s32[]{:S(2)}) async-start(), calls=%async_computation.2 | async-start | bytes 4456448 | tf_op jit(solution)/shard_map/reduce_scatter | solution.py:135
  103.2 9.5 %copy-start.8 = (s32[1,1024,2]{1,2,0:T(2,128)S(1)}, s32[1,1024,2]{1,2,0:T(2,128)}, u32[]{:S(2)}) copy-start(s32[1,1024,2]{1,2,0:T(2,128)} %param.18) | copy-start | bytes 24580
  110.9 4.0 collective-permute-start
  143.9 8.6 %copy-start.5 = (s32[16,64]{1,0:T(8,128)S(1)}, s32[16,64]{1,0:T(8,128)}, u32[]{:S(2)}) copy-start(s32[16,64]{1,0:T(8,128)} %copy-done.4) | copy-start | bytes 12292 | tf_op jit(solution)/shard_map/while
  143.9 8.6 %copy-start.7 = (s32[16,64]{1,0:T(8,128)S(1)}, s32[16,64]{1,0:T(8,128)}, u32[]{:S(2)}) copy-start(s32[16,64]{1,0:T(8,128)} %copy-done.6) | copy-start | bytes 12292 | tf_op jit(solution)/shard_map/while
  143.9 10.1 %copy-start = (f32[192,512]{1,0:T(8,128)S(1)}, f32[192,512]{1,0:T(8,128)}, u32[]{:S(2)}) copy-start(f32[192,512]{1,0:T(8,128)} %get-tuple-element.382) | copy-start | bytes 1179652 | tf_op jit(solution)/shard_map/while
  181.7 8.6 %copy-start.5 = (s32[16,64]{1,0:T(8,128)S(1)}, s32[16,64]{1,0:T(8,128)}, u32[]{:S(2)}) copy-start(s32[16,64]{1,0:T(8,128)} %copy-done.4) | copy-start | bytes 12292 | tf_op jit(solution)/shard_map/while
  181.8 8.6 %copy-start.7 = (s32[16,64]{1,0:T(8,128)S(1)}, s32[16,64]{1,0:T(8,128)}, u32[]{:S(2)}) copy-start(s32[16,64]{1,0:T(8,128)} %copy-done.6) | copy-start | bytes 12292 | tf_op jit(solution)/shard_map/while
  181.8 10.1 %copy-start = (f32[192,512]{1,0:T(8,128)S(1)}, f32[192,512]{1,0:T(8,128)}, u32[]{:S(2)}) copy-start(f32[192,512]{1,0:T(8,128)} %get-tuple-element.382) | copy-start | bytes 1179652 | tf_op jit(solution)/shard_map/while
  219.6 8.6 %copy-start.5 = (s32[16,64]{1,0:T(8,128)S(1)}, s32[16,64]{1,0:T(8,128)}, u32[]{:S(2)}) copy-start(s32[16,64]{1,0:T(8,128)} %copy-done.4) | copy-start | bytes 12292 | tf_op jit(solution)/shard_map/while
  219.6 8.6 %copy-start.7 = (s32[16,64]{1,0:T(8,128)S(1)}, s32[16,64]{1,0:T(8,128)}, u32[]{:S(2)}) copy-start(s32[16,64]{1,0:T(8,128)} %copy-done.6) | copy-start | bytes 12292 | tf_op jit(solution)/shard_map/while
  219.6 10.1 %copy-start = (f32[192,512]{1,0:T(8,128)S(1)}, f32[192,512]{1,0:T(8,128)}, u32[]{:S(2)}) copy-start(f32[192,512]{1,0:T(8,128)} %get-tuple-element.382) | copy-start | bytes 1179652 | tf_op jit(solution)/shard_map/while
  257.5 8.6 %copy-start.5 = (s32[16,64]{1,0:T(8,128)S(1)}, s32[16,64]{1,0:T(8,128)}, u32[]{:S(2)}) copy-start(s32[16,64]{1,0:T(8,128)} %copy-done.4) | copy-start | bytes 12292 | tf_op jit(solution)/shard_map/while
  257.5 8.6 %copy-start.7 = (s32[16,64]{1,0:T(8,128)S(1)}, s32[16,64]{1,0:T(8,128)}, u32[]{:S(2)}) copy-start(s32[16,64]{1,0:T(8,128)} %copy-done.6) | copy-start | bytes 12292 | tf_op jit(solution)/shard_map/while
  257.5 10.1 %copy-start = (f32[192,512]{1,0:T(8,128)S(1)}, f32[192,512]{1,0:T(8,128)}, u32[]{:S(2)}) copy-start(f32[192,512]{1,0:T(8,128)} %get-tuple-element.382) | copy-start | bytes 1179652 | tf_op jit(solution)/shard_map/while
  295.4 8.6 %copy-start.5 = (s32[16,64]{1,0:T(8,128)S(1)}, s32[16,64]{1,0:T(8,128)}, u32[]{:S(2)}) copy-start(s32[16,64]{1,0:T(8,128)} %copy-done.4) | copy-start | bytes 12292 | tf_op jit(solution)/shard_map/while
  295.4 8.6 %copy-start.7 = (s32[16,64]{1,0:T(8,128)S(1)}, s32[16,64]{1,0:T(8,128)}, u32[]{:S(2)}) copy-start(s32[16,64]{1,0:T(8,128)} %copy-done.6) | copy-start | bytes 12292 | tf_op jit(solution)/shard_map/while
  295.4 10.1 %copy-start = (f32[192,512]{1,0:T(8,128)S(1)}, f32[192,512]{1,0:T(8,128)}, u32[]{:S(2)}) copy-start(f32[192,512]{1,0:T(8,128)} %get-tuple-element.382) | copy-start | bytes 1179652 | tf_op jit(solution)/shard_map/while
  333.3 8.6 %copy-start.5 = (s32[16,64]{1,0:T(8,128)S(1)}, s32[16,64]{1,0:T(8,128)}, u32[]{:S(2)}) copy-start(s32[16,64]{1,0:T(8,128)} %copy-done.4) | copy-start | bytes 12292 | tf_op jit(solution)/shard_map/while
  333.3 8.6 %copy-start.7 = (s32[16,64]{1,0:T(8,128)S(1)}, s32[16,64]{1,0:T(8,128)}, u32[]{:S(2)}) copy-start(s32[16,64]{1,0:T(8,128)} %copy-done.6) | copy-start | bytes 12292 | tf_op jit(solution)/shard_map/while
  333.3 10.1 %copy-start = (f32[192,512]{1,0:T(8,128)S(1)}, f32[192,512]{1,0:T(8,128)}, u32[]{:S(2)}) copy-start(f32[192,512]{1,0:T(8,128)} %get-tuple-element.382) | copy-start | bytes 1179652 | tf_op jit(solution)/shard_map/while
  371.1 8.6 %copy-start.5 = (s32[16,64]{1,0:T(8,128)S(1)}, s32[16,64]{1,0:T(8,128)}, u32[]{:S(2)}) copy-start(s32[16,64]{1,0:T(8,128)} %copy-done.4) | copy-start | bytes 12292 | tf_op jit(solution)/shard_map/while
  371.2 8.6 %copy-start.7 = (s32[16,64]{1,0:T(8,128)S(1)}, s32[16,64]{1,0:T(8,128)}, u32[]{:S(2)}) copy-start(s32[16,64]{1,0:T(8,128)} %copy-done.6) | copy-start | bytes 12292 | tf_op jit(solution)/shard_map/while
  371.2 10.1 %copy-start = (f32[192,512]{1,0:T(8,128)S(1)}, f32[192,512]{1,0:T(8,128)}, u32[]{:S(2)}) copy-start(f32[192,512]{1,0:T(8,128)} %get-tuple-element.382) | copy-start | bytes 1179652 | tf_op jit(solution)/shard_map/while
  409.0 8.6 %copy-start.5 = (s32[16,64]{1,0:T(8,128)S(1)}, s32[16,64]{1,0:T(8,128)}, u32[]{:S(2)}) copy-start(s32[16,64]{1,0:T(8,128)} %copy-done.4) | copy-start | bytes 12292 | tf_op jit(solution)/shard_map/while
  409.0 8.6 %copy-start.7 = (s32[16,64]{1,0:T(8,128)S(1)}, s32[16,64]{1,0:T(8,128)}, u32[]{:S(2)}) copy-start(s32[16,64]{1,0:T(8,128)} %copy-done.6) | copy-start | bytes 12292 | tf_op jit(solution)/shard_map/while
  409.0 10.1 %copy-start = (f32[192,512]{1,0:T(8,128)S(1)}, f32[192,512]{1,0:T(8,128)}, u32[]{:S(2)}) copy-start(f32[192,512]{1,0:T(8,128)} %get-tuple-element.382) | copy-start | bytes 1179652 | tf_op jit(solution)/shard_map/while
  446.9 8.6 %copy-start.5 = (s32[16,64]{1,0:T(8,128)S(1)}, s32[16,64]{1,0:T(8,128)}, u32[]{:S(2)}) copy-start(s32[16,64]{1,0:T(8,128)} %copy-done.4) | copy-start | bytes 12292 | tf_op jit(solution)/shard_map/while
  446.9 8.6 %copy-start.7 = (s32[16,64]{1,0:T(8,128)S(1)}, s32[16,64]{1,0:T(8,128)}, u32[]{:S(2)}) copy-start(s32[16,64]{1,0:T(8,128)} %copy-done.6) | copy-start | bytes 12292 | tf_op jit(solution)/shard_map/while
  446.9 10.1 %copy-start = (f32[192,512]{1,0:T(8,128)S(1)}, f32[192,512]{1,0:T(8,128)}, u32[]{:S(2)}) copy-start(f32[192,512]{1,0:T(8,128)} %get-tuple-element.382) | copy-start | bytes 1179652 | tf_op jit(solution)/shard_map/while
  484.8 8.6 %copy-start.5 = (s32[16,64]{1,0:T(8,128)S(1)}, s32[16,64]{1,0:T(8,128)}, u32[]{:S(2)}) copy-start(s32[16,64]{1,0:T(8,128)} %copy-done.4) | copy-start | bytes 12292 | tf_op jit(solution)/shard_map/while
  484.8 8.6 %copy-start.7 = (s32[16,64]{1,0:T(8,128)S(1)}, s32[16,64]{1,0:T(8,128)}, u32[]{:S(2)}) copy-start(s32[16,64]{1,0:T(8,128)} %copy-done.6) | copy-start | bytes 12292 | tf_op jit(solution)/shard_map/while
  484.8 10.1 %copy-start = (f32[192,512]{1,0:T(8,128)S(1)}, f32[192,512]{1,0:T(8,128)}, u32[]{:S(2)}) copy-start(f32[192,512]{1,0:T(8,128)} %get-tuple-element.382) | copy-start | bytes 1179652 | tf_op jit(solution)/shard_map/while
  522.7 8.6 %copy-start.5 = (s32[16,64]{1,0:T(8,128)S(1)}, s32[16,64]{1,0:T(8,128)}, u32[]{:S(2)}) copy-start(s32[16,64]{1,0:T(8,128)} %copy-done.4) | copy-start | bytes 12292 | tf_op jit(solution)/shard_map/while
  522.7 8.6 %copy-start.7 = (s32[16,64]{1,0:T(8,128)S(1)}, s32[16,64]{1,0:T(8,128)}, u32[]{:S(2)}) copy-start(s32[16,64]{1,0:T(8,128)} %copy-done.6) | copy-start | bytes 12292 | tf_op jit(solution)/shard_map/while
  522.7 10.1 %copy-start = (f32[192,512]{1,0:T(8,128)S(1)}, f32[192,512]{1,0:T(8,128)}, u32[]{:S(2)}) copy-start(f32[192,512]{1,0:T(8,128)} %get-tuple-element.382) | copy-start | bytes 1179652 | tf_op jit(solution)/shard_map/while
  560.5 8.6 %copy-start.5 = (s32[16,64]{1,0:T(8,128)S(1)}, s32[16,64]{1,0:T(8,128)}, u32[]{:S(2)}) copy-start(s32[16,64]{1,0:T(8,128)} %copy-done.4) | copy-start | bytes 12292 | tf_op jit(solution)/shard_map/while
  560.6 8.6 %copy-start.7 = (s32[16,64]{1,0:T(8,128)S(1)}, s32[16,64]{1,0:T(8,128)}, u32[]{:S(2)}) copy-start(s32[16,64]{1,0:T(8,128)} %copy-done.6) | copy-start | bytes 12292 | tf_op jit(solution)/shard_map/while
  560.6 10.1 %copy-start = (f32[192,512]{1,0:T(8,128)S(1)}, f32[192,512]{1,0:T(8,128)}, u32[]{:S(2)}) copy-start(f32[192,512]{1,0:T(8,128)} %get-tuple-element.382) | copy-start | bytes 1179652 | tf_op jit(solution)/shard_map/while
  598.4 8.6 %copy-start.5 = (s32[16,64]{1,0:T(8,128)S(1)}, s32[16,64]{1,0:T(8,128)}, u32[]{:S(2)}) copy-start(s32[16,64]{1,0:T(8,128)} %copy-done.4) | copy-start | bytes 12292 | tf_op jit(solution)/shard_map/while
  598.4 8.6 %copy-start.7 = (s32[16,64]{1,0:T(8,128)S(1)}, s32[16,64]{1,0:T(8,128)}, u32[]{:S(2)}) copy-start(s32[16,64]{1,0:T(8,128)} %copy-done.6) | copy-start | bytes 12292 | tf_op jit(solution)/shard_map/while
  598.4 10.1 %copy-start = (f32[192,512]{1,0:T(8,128)S(1)}, f32[192,512]{1,0:T(8,128)}, u32[]{:S(2)}) copy-start(f32[192,512]{1,0:T(8,128)} %get-tuple-element.382) | copy-start | bytes 1179652 | tf_op jit(solution)/shard_map/while
  636.3 8.6 %copy-start.5 = (s32[16,64]{1,0:T(8,128)S(1)}, s32[16,64]{1,0:T(8,128)}, u32[]{:S(2)}) copy-start(s32[16,64]{1,0:T(8,128)} %copy-done.4) | copy-start | bytes 12292 | tf_op jit(solution)/shard_map/while
  636.3 10.1 %copy-start = (f32[192,512]{1,0:T(8,128)S(1)}, f32[192,512]{1,0:T(8,128)}, u32[]{:S(2)}) copy-start(f32[192,512]{1,0:T(8,128)} %get-tuple-element.382) | copy-start | bytes 1179652 | tf_op jit(solution)/shard_map/while
  674.2 10.1 %copy-start = (f32[192,512]{1,0:T(8,128)S(1)}, f32[192,512]{1,0:T(8,128)}, u32[]{:S(2)}) copy-start(f32[192,512]{1,0:T(8,128)} %get-tuple-element.382) | copy-start | bytes 1179652 | tf_op jit(solution)/shard_map/while
  712.1 10.1 %copy-start = (f32[192,512]{1,0:T(8,128)S(1)}, f32[192,512]{1,0:T(8,128)}, u32[]{:S(2)}) copy-start(f32[192,512]{1,0:T(8,128)} %get-tuple-element.382) | copy-start | bytes 1179652 | tf_op jit(solution)/shard_map/while
  723.4 12.9 %collective-permute-start.1 = (f32[192,512]{1,0:T(8,128)S(1)}, f32[192,512]{1,0:T(8,128)S(1)}, u32[]{:S(2)}, u32[]{:S(2)}) collective-permute-start(f32[192,512]{1,0:T(8,128)S(1)} %slice.109), channel_id=1, source_target_pairs={{16,0},{32,16},{48,32},{64,48},{80,64},{96,80},{112,96},{17,1},{33... | collective-permute-start | bytes 1179656 | tf_op jit(solution)/shard_map/ppermute | solution.py:15
  (70 other events, 176.8 us)
Sparse Core Ops, SparseCore 0:
  12.0 78.4 all-gather.1
  741.4 83.3 reduce-scatter.1
where the time goes:
time: 836 us; the launch traced here: 833 us
  other arithmetic  564 us (67%)
  local copies, waits for them, and re-layouts  123 us (15%)
  waiting for transfers between devices  76 us (9%)
  blocking collectives  25.4 us (3%)
  matrix products  23.4 us (3%)
  between operations  14.2 us (2%)
    reduce_sum x16, other arithmetic, tile_pair(): jnp.sum(viscous - conduct, 0)[None]  147 us
    reduce_sum x16, other arithmetic, tile_pair(): jnp.sum(force, 1)  135 us
    reduce_sum x16, other arithmetic, tile_pair(): along = jnp.sum(unit * relative, 0)  128 us
    reduce_sum x16, other arithmetic, tile_pair(): radius = jnp.sqrt(jnp.sum(offset * offset, 0) + 0.01)  66.2 us
    all_gather x1, waiting for transfers between devices, per_device(): group_data = lax.all_gather(owned, 'tile', axis=0, tiled=True)  50.3 us
    gather x16, local copies, waits for them, and re-layouts, consume(): reachable[second_index]  39.7 us
    all_gather x1, blocking collectives, per_device(): tables = lax.all_gather(exported_tile_places, 'tile', axis=0, tiled=True)  25.4 us
    mul x8, other arithmetic, tile_self(): (repulse * weight - friction * weight * weight * along + noise_amp * weig...  19.2 us
  transfers between devices with their start and end apart: 4, of which 4 were waited for; matrix products, arithmetic and copies ran while one was open for 9% of the time, Pallas kernels for 0%

commit v1 on v0

--- a/solution.py
+++ b/solution.py
@@ -93,7 +93,19 @@
     )
     owned = owned.reshape(9, blocks, 128).transpose(1, 0, 2)
     group_data = lax.all_gather(owned, "tile", axis=0, tiled=True)
-    tables = lax.all_gather(exported_tile_places, "tile", axis=0, tiled=True)
+    world_n = lax.axis_size("tile")
+    arrivals = tuple(((k, (k + 1) % world_n) for k in range(world_n)))
+    cards = tuple(((k, (k - 1) % world_n) for k in range(world_n)))
+    r2, v1 = ([exported_tile_places], [exported_tile_places])
+    for _ in range(world_n // 2):
+        r2.append(lax.ppermute(r2[-1], axis_name="tile", perm=arrivals))
+    for _ in range((world_n - 1) // 2):
+        v1.append(lax.ppermute(v1[-1], "tile", perm=cards))
+    tables = jnp.roll(
+        jnp.concatenate([*r2[::-1], *v1[1:]], 0),
+        (lax.axis_index("tile") - world_n // 2) * exported_tile_places.shape[0],
+        0,
+    )
     my_index = lax.axis_index("tile")
     my_slots = lax.dynamic_index_in_dim(tables, my_index, 1, keepdims=False)
     group_ids = (jnp.arange(n_tile, dtype=jnp.int32)[:, None] * blocks + my_slots).reshape(-1)

time: 836 us -> 835 us (level)
  starting transfers between devices: 3.3 us -> 43.5 us
  blocking collectives: 25.4 us -> 0 us
  waiting for transfers between devices: 76 us -> 61.6 us
    ppermute x0 -> x15, starting transfers between devices: none -> 40 us  [the longest x7 37.9 us: per_device(): v1.append(lax.ppermute(v1[-1], 'tile', perm=cards))]
    all_gather x1, waiting for transfers between devices: 50.3 us -> 19.3 us  [per_device(): group_data = lax.all_gather(owned, 'tile', axis=0, tiled=True)]
    all_gather x1 -> x0, blocking collectives: 25.4 us -> none  [per_device(): tables = lax.all_gather(exported_tile_places, 'tile', axis=0, tiled=True)]
    ppermute x0 -> x15, waiting for transfers between devices: none -> 17.2 us  [the longest x8 17.2 us: per_device(): r2.append(lax.ppermute(r2[-1], axis_name='tile', perm=arrivals))]
  transfers between devices with their start and end apart: 4 -> 19, of which waited for: 4 -> 12; matrix products, arithmetic and copies ran while one was open for 9% -> 9% of each run, Pallas kernels for 0% -> 0%
where the time goes in v1:
time: 835 us; the launch traced here: 833 us
  other arithmetic  564 us (68%)
  local copies, waits for them, and re-layouts  122 us (15%)
  waiting for transfers between devices  61.6 us (7%)
  starting transfers between devices  43.5 us (5%)
  matrix products  23.4 us (3%)
  between operations  14.2 us (2%)
    reduce_sum x16, other arithmetic, tile_pair(): jnp.sum(viscous - conduct, 0)[None]  147 us
    reduce_sum x16, other arithmetic, tile_pair(): jnp.sum(force, 1)  135 us
    reduce_sum x16, other arithmetic, tile_pair(): along = jnp.sum(unit * relative, 0)  128 us
    reduce_sum x16, other arithmetic, tile_pair(): radius = jnp.sqrt(jnp.sum(offset * offset, 0) + 0.01)  66.2 us
    gather x16, local copies, waits for them, and re-layouts, consume(): reachable[second_index]  39.7 us
    ppermute x7, starting transfers between devices, per_device(): v1.append(lax.ppermute(v1[-1], 'tile', perm=cards))  37.9 us
    all_gather x1, waiting for transfers between devices, per_device(): group_data = lax.all_gather(owned, 'tile', axis=0, tiled=True)  19.3 us
    mul x8, other arithmetic, tile_self(): (repulse * weight - friction * weight * weight * along + noise_amp * weig...  19.2 us
  transfers between devices with their start and end apart: 19, of which 12 were waited for; matrix products, arithmetic and copies ran while one was open for 9% of the time, Pallas kernels for 0%

profile of v1, /device:TPU:0, one launch (start us, length us, event | category | flops | bytes accessed | tf_op | source)
XLA Modules:
  0.0 833.0 jit_solution(13755779693994445033)
XLA Ops:
  71.5 19.3 %all-gather.2.cloned.1.call-done = f32[2048,9,128]{2,0,1:T(8,128)} async-done(((f32[128,9,128]{2,0,1:T(8,128)}), f32[2048,9,128]{2,0,1:T(8,128)}) %all-gather.2.cloned.1.call-update) | async-done | bytes 9437200 | tf_op jit(solution)/shard_map/all_gather | solution.py:95
  90.7 12.7 %copy.36 = f32[2048,9,128]{2,1,0:T(8,128)} copy(f32[2048,9,128]{2,0,1:T(8,128)} %all-gather.2.cloned.1.call-done) | data formatting | bytes 18874368 | tf_op jit(solution)/shard_map/all_gather | solution.py:95
  117.6 605.7 %while.28 = (s32[]{:T(128)}, f32[192,512]{1,0:T(8,128)}, f32[384,512]{1,0:T(8,128)S(1)}, s32[16,64]{1,0:T(8,128)S(1)}, f32[192,9,128]{2,1,0:T(8,128)S(1)}, /*ind...) while((s32[]{:T(128)}, f32[192,512]{1,0:T(8,128)}, ...), condition=%wide.region_7.8_spmd.clone, body=%wide.region_0.7_spmd.clone.sunk | while | flops 305871232 | bytes 52507452 | solution.py:143
  126.7 8.0 multiply_reduce_fusion.11
  134.9 9.2 %subtract_reduce_fusion.2 = (f32[64,128]{1,0:T(8,128)S(1)}, f32[64,128]{1,0:T(8,128)S(1)}, f32[64,128,128]{2,1,0:T(8,128)S(1)}) fusion(f32[64,128,128]{2,1,0:T(8,128)S(1)} %multiply_reduce_fusion.11, f32[64,128]{1,0:T(8,128)S(1)} %bitcast.118, f32[64,128]{1,0:T(8,128)S(1)} %bitcast.121, f32[64,128,128]{2,1,0:T(8,128)S(1)} %fusion.71, ...), kind=kLoop, calls=%fused_computation.59.clone.1 | loop fusion | flops 38780928 | bytes 12845056 | tf_op jit(solution)/shard_map/while/body/eval_jaxpr/vmap()/reduce_sum | solution.py:37
  144.1 8.5 %multiply_reduce_fusion.12 = (f32[64,3,128]{2,1,0:T(4,128)S(1)}, f32[64,3,128]{2,1,0:T(4,128)S(1)}) fusion(f32[64,128,128]{2,1,0:T(8,128)S(1)} %get-tuple-element.363, f32[64,128,128]{2,1,0:T(8,128)S(1)} %add_sqrt_fusion.5, f32[64,3,128]{2,1,0:T(4,128)S(1)} %get-tuple-element.354, f32[64,3,128]{2,1,0:T(4,128)S(1)} %get-tuple-element.355), kind=kLoop, calls=%fused_computation.44.clone.1 | loop fusion | flops 15679488 | bytes 8781824 | tf_op jit(solution)/shard_map/while/body/eval_jaxpr/vmap()/reduce_sum | solution.py:37
  164.6 8.0 multiply_reduce_fusion.11
  172.8 9.2 %subtract_reduce_fusion.2 = (f32[64,128]{1,0:T(8,128)S(1)}, f32[64,128]{1,0:T(8,128)S(1)}, f32[64,128,128]{2,1,0:T(8,128)S(1)}) fusion(f32[64,128,128]{2,1,0:T(8,128)S(1)} %multiply_reduce_fusion.11, f32[64,128]{1,0:T(8,128)S(1)} %bitcast.118, f32[64,128]{1,0:T(8,128)S(1)} %bitcast.121, f32[64,128,128]{2,1,0:T(8,128)S(1)} %fusion.71, ...), kind=kLoop, calls=%fused_computation.59.clone.1 | loop fusion | flops 38780928 | bytes 12845056 | tf_op jit(solution)/shard_map/while/body/eval_jaxpr/vmap()/reduce_sum | solution.py:37
  182.0 8.5 %multiply_reduce_fusion.12 = (f32[64,3,128]{2,1,0:T(4,128)S(1)}, f32[64,3,128]{2,1,0:T(4,128)S(1)}) fusion(f32[64,128,128]{2,1,0:T(8,128)S(1)} %get-tuple-element.363, f32[64,128,128]{2,1,0:T(8,128)S(1)} %add_sqrt_fusion.5, f32[64,3,128]{2,1,0:T(4,128)S(1)} %get-tuple-element.354, f32[64,3,128]{2,1,0:T(4,128)S(1)} %get-tuple-element.355), kind=kLoop, calls=%fused_computation.44.clone.1 | loop fusion | flops 15679488 | bytes 8781824 | tf_op jit(solution)/shard_map/while/body/eval_jaxpr/vmap()/reduce_sum | solution.py:37
  202.4 8.0 multiply_reduce_fusion.11
  210.6 9.2 %subtract_reduce_fusion.2 = (f32[64,128]{1,0:T(8,128)S(1)}, f32[64,128]{1,0:T(8,128)S(1)}, f32[64,128,128]{2,1,0:T(8,128)S(1)}) fusion(f32[64,128,128]{2,1,0:T(8,128)S(1)} %multiply_reduce_fusion.11, f32[64,128]{1,0:T(8,128)S(1)} %bitcast.118, f32[64,128]{1,0:T(8,128)S(1)} %bitcast.121, f32[64,128,128]{2,1,0:T(8,128)S(1)} %fusion.71, ...), kind=kLoop, calls=%fused_computation.59.clone.1 | loop fusion | flops 38780928 | bytes 12845056 | tf_op jit(solution)/shard_map/while/body/eval_jaxpr/vmap()/reduce_sum | solution.py:37
  219.8 8.5 %multiply_reduce_fusion.12 = (f32[64,3,128]{2,1,0:T(4,128)S(1)}, f32[64,3,128]{2,1,0:T(4,128)S(1)}) fusion(f32[64,128,128]{2,1,0:T(8,128)S(1)} %get-tuple-element.363, f32[64,128,128]{2,1,0:T(8,128)S(1)} %add_sqrt_fusion.5, f32[64,3,128]{2,1,0:T(4,128)S(1)} %get-tuple-element.354, f32[64,3,128]{2,1,0:T(4,128)S(1)} %get-tuple-element.355), kind=kLoop, calls=%fused_computation.44.clone.1 | loop fusion | flops 15679488 | bytes 8781824 | tf_op jit(solution)/shard_map/while/body/eval_jaxpr/vmap()/reduce_sum | solution.py:37
  240.3 8.0 multiply_reduce_fusion.11
  248.5 9.2 %subtract_reduce_fusion.2 = (f32[64,128]{1,0:T(8,128)S(1)}, f32[64,128]{1,0:T(8,128)S(1)}, f32[64,128,128]{2,1,0:T(8,128)S(1)}) fusion(f32[64,128,128]{2,1,0:T(8,128)S(1)} %multiply_reduce_fusion.11, f32[64,128]{1,0:T(8,128)S(1)} %bitcast.118, f32[64,128]{1,0:T(8,128)S(1)} %bitcast.121, f32[64,128,128]{2,1,0:T(8,128)S(1)} %fusion.71, ...), kind=kLoop, calls=%fused_computation.59.clone.1 | loop fusion | flops 38780928 | bytes 12845056 | tf_op jit(solution)/shard_map/while/body/eval_jaxpr/vmap()/reduce_sum | solution.py:37
  257.7 8.5 %multiply_reduce_fusion.12 = (f32[64,3,128]{2,1,0:T(4,128)S(1)}, f32[64,3,128]{2,1,0:T(4,128)S(1)}) fusion(f32[64,128,128]{2,1,0:T(8,128)S(1)} %get-tuple-element.363, f32[64,128,128]{2,1,0:T(8,128)S(1)} %add_sqrt_fusion.5, f32[64,3,128]{2,1,0:T(4,128)S(1)} %get-tuple-element.354, f32[64,3,128]{2,1,0:T(4,128)S(1)} %get-tuple-element.355), kind=kLoop, calls=%fused_computation.44.clone.1 | loop fusion | flops 15679488 | bytes 8781824 | tf_op jit(solution)/shard_map/while/body/eval_jaxpr/vmap()/reduce_sum | solution.py:37
  278.1 8.0 multiply_reduce_fusion.11
  286.3 9.2 %subtract_reduce_fusion.2 = (f32[64,128]{1,0:T(8,128)S(1)}, f32[64,128]{1,0:T(8,128)S(1)}, f32[64,128,128]{2,1,0:T(8,128)S(1)}) fusion(f32[64,128,128]{2,1,0:T(8,128)S(1)} %multiply_reduce_fusion.11, f32[64,128]{1,0:T(8,128)S(1)} %bitcast.118, f32[64,128]{1,0:T(8,128)S(1)} %bitcast.121, f32[64,128,128]{2,1,0:T(8,128)S(1)} %fusion.71, ...), kind=kLoop, calls=%fused_computation.59.clone.1 | loop fusion | flops 38780928 | bytes 12845056 | tf_op jit(solution)/shard_map/while/body/eval_jaxpr/vmap()/reduce_sum | solution.py:37
  295.5 8.5 %multiply_reduce_fusion.12 = (f32[64,3,128]{2,1,0:T(4,128)S(1)}, f32[64,3,128]{2,1,0:T(4,128)S(1)}) fusion(f32[64,128,128]{2,1,0:T(8,128)S(1)} %get-tuple-element.363, f32[64,128,128]{2,1,0:T(8,128)S(1)} %add_sqrt_fusion.5, f32[64,3,128]{2,1,0:T(4,128)S(1)} %get-tuple-element.354, f32[64,3,128]{2,1,0:T(4,128)S(1)} %get-tuple-element.355), kind=kLoop, calls=%fused_computation.44.clone.1 | loop fusion | flops 15679488 | bytes 8781824 | tf_op jit(solution)/shard_map/while/body/eval_jaxpr/vmap()/reduce_sum | solution.py:37
  316.0 8.0 multiply_reduce_fusion.11
  324.2 9.2 %subtract_reduce_fusion.2 = (f32[64,128]{1,0:T(8,128)S(1)}, f32[64,128]{1,0:T(8,128)S(1)}, f32[64,128,128]{2,1,0:T(8,128)S(1)}) fusion(f32[64,128,128]{2,1,0:T(8,128)S(1)} %multiply_reduce_fusion.11, f32[64,128]{1,0:T(8,128)S(1)} %bitcast.118, f32[64,128]{1,0:T(8,128)S(1)} %bitcast.121, f32[64,128,128]{2,1,0:T(8,128)S(1)} %fusion.71, ...), kind=kLoop, calls=%fused_computation.59.clone.1 | loop fusion | flops 38780928 | bytes 12845056 | tf_op jit(solution)/shard_map/while/body/eval_jaxpr/vmap()/reduce_sum | solution.py:37
  333.4 8.5 %multiply_reduce_fusion.12 = (f32[64,3,128]{2,1,0:T(4,128)S(1)}, f32[64,3,128]{2,1,0:T(4,128)S(1)}) fusion(f32[64,128,128]{2,1,0:T(8,128)S(1)} %get-tuple-element.363, f32[64,128,128]{2,1,0:T(8,128)S(1)} %add_sqrt_fusion.5, f32[64,3,128]{2,1,0:T(4,128)S(1)} %get-tuple-element.354, f32[64,3,128]{2,1,0:T(4,128)S(1)} %get-tuple-element.355), kind=kLoop, calls=%fused_computation.44.clone.1 | loop fusion | flops 15679488 | bytes 8781824 | tf_op jit(solution)/shard_map/while/body/eval_jaxpr/vmap()/reduce_sum | solution.py:37
  362.0 9.2 %subtract_reduce_fusion.2 = (f32[64,128]{1,0:T(8,128)S(1)}, f32[64,128]{1,0:T(8,128)S(1)}, f32[64,128,128]{2,1,0:T(8,128)S(1)}) fusion(f32[64,128,128]{2,1,0:T(8,128)S(1)} %multiply_reduce_fusion.11, f32[64,128]{1,0:T(8,128)S(1)} %bitcast.118, f32[64,128]{1,0:T(8,128)S(1)} %bitcast.121, f32[64,128,128]{2,1,0:T(8,128)S(1)} %fusion.71, ...), kind=kLoop, calls=%fused_computation.59.clone.1 | loop fusion | flops 38780928 | bytes 12845056 | tf_op jit(solution)/shard_map/while/body/eval_jaxpr/vmap()/reduce_sum | solution.py:37
  371.2 8.5 %multiply_reduce_fusion.12 = (f32[64,3,128]{2,1,0:T(4,128)S(1)}, f32[64,3,128]{2,1,0:T(4,128)S(1)}) fusion(f32[64,128,128]{2,1,0:T(8,128)S(1)} %get-tuple-element.363, f32[64,128,128]{2,1,0:T(8,128)S(1)} %add_sqrt_fusion.5, f32[64,3,128]{2,1,0:T(4,128)S(1)} %get-tuple-element.354, f32[64,3,128]{2,1,0:T(4,128)S(1)} %get-tuple-element.355), kind=kLoop, calls=%fused_computation.44.clone.1 | loop fusion | flops 15679488 | bytes 8781824 | tf_op jit(solution)/shard_map/while/body/eval_jaxpr/vmap()/reduce_sum | solution.py:37
  391.7 8.0 multiply_reduce_fusion.11
  399.9 9.2 %subtract_reduce_fusion.2 = (f32[64,128]{1,0:T(8,128)S(1)}, f32[64,128]{1,0:T(8,128)S(1)}, f32[64,128,128]{2,1,0:T(8,128)S(1)}) fusion(f32[64,128,128]{2,1,0:T(8,128)S(1)} %multiply_reduce_fusion.11, f32[64,128]{1,0:T(8,128)S(1)} %bitcast.118, f32[64,128]{1,0:T(8,128)S(1)} %bitcast.121, f32[64,128,128]{2,1,0:T(8,128)S(1)} %fusion.71, ...), kind=kLoop, calls=%fused_computation.59.clone.1 | loop fusion | flops 38780928 | bytes 12845056 | tf_op jit(solution)/shard_map/while/body/eval_jaxpr/vmap()/reduce_sum | solution.py:37
  409.1 8.5 %multiply_reduce_fusion.12 = (f32[64,3,128]{2,1,0:T(4,128)S(1)}, f32[64,3,128]{2,1,0:T(4,128)S(1)}) fusion(f32[64,128,128]{2,1,0:T(8,128)S(1)} %get-tuple-element.363, f32[64,128,128]{2,1,0:T(8,128)S(1)} %add_sqrt_fusion.5, f32[64,3,128]{2,1,0:T(4,128)S(1)} %get-tuple-element.354, f32[64,3,128]{2,1,0:T(4,128)S(1)} %get-tuple-element.355), kind=kLoop, calls=%fused_computation.44.clone.1 | loop fusion | flops 15679488 | bytes 8781824 | tf_op jit(solution)/shard_map/while/body/eval_jaxpr/vmap()/reduce_sum | solution.py:37
  429.5 8.0 multiply_reduce_fusion.11
  437.7 9.2 %subtract_reduce_fusion.2 = (f32[64,128]{1,0:T(8,128)S(1)}, f32[64,128]{1,0:T(8,128)S(1)}, f32[64,128,128]{2,1,0:T(8,128)S(1)}) fusion(f32[64,128,128]{2,1,0:T(8,128)S(1)} %multiply_reduce_fusion.11, f32[64,128]{1,0:T(8,128)S(1)} %bitcast.118, f32[64,128]{1,0:T(8,128)S(1)} %bitcast.121, f32[64,128,128]{2,1,0:T(8,128)S(1)} %fusion.71, ...), kind=kLoop, calls=%fused_computation.59.clone.1 | loop fusion | flops 38780928 | bytes 12845056 | tf_op jit(solution)/shard_map/while/body/eval_jaxpr/vmap()/reduce_sum | solution.py:37
  446.9 8.5 %multiply_reduce_fusion.12 = (f32[64,3,128]{2,1,0:T(4,128)S(1)}, f32[64,3,128]{2,1,0:T(4,128)S(1)}) fusion(f32[64,128,128]{2,1,0:T(8,128)S(1)} %get-tuple-element.363, f32[64,128,128]{2,1,0:T(8,128)S(1)} %add_sqrt_fusion.5, f32[64,3,128]{2,1,0:T(4,128)S(1)} %get-tuple-element.354, f32[64,3,128]{2,1,0:T(4,128)S(1)} %get-tuple-element.355), kind=kLoop, calls=%fused_computation.44.clone.1 | loop fusion | flops 15679488 | bytes 8781824 | tf_op jit(solution)/shard_map/while/body/eval_jaxpr/vmap()/reduce_sum | solution.py:37
  467.4 8.0 multiply_reduce_fusion.11
  475.6 9.2 %subtract_reduce_fusion.2 = (f32[64,128]{1,0:T(8,128)S(1)}, f32[64,128]{1,0:T(8,128)S(1)}, f32[64,128,128]{2,1,0:T(8,128)S(1)}) fusion(f32[64,128,128]{2,1,0:T(8,128)S(1)} %multiply_reduce_fusion.11, f32[64,128]{1,0:T(8,128)S(1)} %bitcast.118, f32[64,128]{1,0:T(8,128)S(1)} %bitcast.121, f32[64,128,128]{2,1,0:T(8,128)S(1)} %fusion.71, ...), kind=kLoop, calls=%fused_computation.59.clone.1 | loop fusion | flops 38780928 | bytes 12845056 | tf_op jit(solution)/shard_map/while/body/eval_jaxpr/vmap()/reduce_sum | solution.py:37
  484.8 8.5 %multiply_reduce_fusion.12 = (f32[64,3,128]{2,1,0:T(4,128)S(1)}, f32[64,3,128]{2,1,0:T(4,128)S(1)}) fusion(f32[64,128,128]{2,1,0:T(8,128)S(1)} %get-tuple-element.363, f32[64,128,128]{2,1,0:T(8,128)S(1)} %add_sqrt_fusion.5, f32[64,3,128]{2,1,0:T(4,128)S(1)} %get-tuple-element.354, f32[64,3,128]{2,1,0:T(4,128)S(1)} %get-tuple-element.355), kind=kLoop, calls=%fused_computation.44.clone.1 | loop fusion | flops 15679488 | bytes 8781824 | tf_op jit(solution)/shard_map/while/body/eval_jaxpr/vmap()/reduce_sum | solution.py:37
  505.3 8.0 multiply_reduce_fusion.11
  513.4 9.2 %subtract_reduce_fusion.2 = (f32[64,128]{1,0:T(8,128)S(1)}, f32[64,128]{1,0:T(8,128)S(1)}, f32[64,128,128]{2,1,0:T(8,128)S(1)}) fusion(f32[64,128,128]{2,1,0:T(8,128)S(1)} %multiply_reduce_fusion.11, f32[64,128]{1,0:T(8,128)S(1)} %bitcast.118, f32[64,128]{1,0:T(8,128)S(1)} %bitcast.121, f32[64,128,128]{2,1,0:T(8,128)S(1)} %fusion.71, ...), kind=kLoop, calls=%fused_computation.59.clone.1 | loop fusion | flops 38780928 | bytes 12845056 | tf_op jit(solution)/shard_map/while/body/eval_jaxpr/vmap()/reduce_sum | solution.py:37
  522.6 8.5 %multiply_reduce_fusion.12 = (f32[64,3,128]{2,1,0:T(4,128)S(1)}, f32[64,3,128]{2,1,0:T(4,128)S(1)}) fusion(f32[64,128,128]{2,1,0:T(8,128)S(1)} %get-tuple-element.363, f32[64,128,128]{2,1,0:T(8,128)S(1)} %add_sqrt_fusion.5, f32[64,3,128]{2,1,0:T(4,128)S(1)} %get-tuple-element.354, f32[64,3,128]{2,1,0:T(4,128)S(1)} %get-tuple-element.355), kind=kLoop, calls=%fused_computation.44.clone.1 | loop fusion | flops 15679488 | bytes 8781824 | tf_op jit(solution)/shard_map/while/body/eval_jaxpr/vmap()/reduce_sum | solution.py:37
  551.3 9.2 %subtract_reduce_fusion.2 = (f32[64,128]{1,0:T(8,128)S(1)}, f32[64,128]{1,0:T(8,128)S(1)}, f32[64,128,128]{2,1,0:T(8,128)S(1)}) fusion(f32[64,128,128]{2,1,0:T(8,128)S(1)} %multiply_reduce_fusion.11, f32[64,128]{1,0:T(8,128)S(1)} %bitcast.118, f32[64,128]{1,0:T(8,128)S(1)} %bitcast.121, f32[64,128,128]{2,1,0:T(8,128)S(1)} %fusion.71, ...), kind=kLoop, calls=%fused_computation.59.clone.1 | loop fusion | flops 38780928 | bytes 12845056 | tf_op jit(solution)/shard_map/while/body/eval_jaxpr/vmap()/reduce_sum | solution.py:37
  560.5 8.5 %multiply_reduce_fusion.12 = (f32[64,3,128]{2,1,0:T(4,128)S(1)}, f32[64,3,128]{2,1,0:T(4,128)S(1)}) fusion(f32[64,128,128]{2,1,0:T(8,128)S(1)} %get-tuple-element.363, f32[64,128,128]{2,1,0:T(8,128)S(1)} %add_sqrt_fusion.5, f32[64,3,128]{2,1,0:T(4,128)S(1)} %get-tuple-element.354, f32[64,3,128]{2,1,0:T(4,128)S(1)} %get-tuple-element.355), kind=kLoop, calls=%fused_computation.44.clone.1 | loop fusion | flops 15679488 | bytes 8781824 | tf_op jit(solution)/shard_map/while/body/eval_jaxpr/vmap()/reduce_sum | solution.py:37
  589.2 9.2 %subtract_reduce_fusion.2 = (f32[64,128]{1,0:T(8,128)S(1)}, f32[64,128]{1,0:T(8,128)S(1)}, f32[64,128,128]{2,1,0:T(8,128)S(1)}) fusion(f32[64,128,128]{2,1,0:T(8,128)S(1)} %multiply_reduce_fusion.11, f32[64,128]{1,0:T(8,128)S(1)} %bitcast.118, f32[64,128]{1,0:T(8,128)S(1)} %bitcast.121, f32[64,128,128]{2,1,0:T(8,128)S(1)} %fusion.71, ...), kind=kLoop, calls=%fused_computation.59.clone.1 | loop fusion | flops 38780928 | bytes 12845056 | tf_op jit(solution)/shard_map/while/body/eval_jaxpr/vmap()/reduce_sum | solution.py:37
  598.4 8.5 %multiply_reduce_fusion.12 = (f32[64,3,128]{2,1,0:T(4,128)S(1)}, f32[64,3,128]{2,1,0:T(4,128)S(1)}) fusion(f32[64,128,128]{2,1,0:T(8,128)S(1)} %get-tuple-element.363, f32[64,128,128]{2,1,0:T(8,128)S(1)} %add_sqrt_fusion.5, f32[64,3,128]{2,1,0:T(4,128)S(1)} %get-tuple-element.354, f32[64,3,128]{2,1,0:T(4,128)S(1)} %get-tuple-element.355), kind=kLoop, calls=%fused_computation.44.clone.1 | loop fusion | flops 15679488 | bytes 8781824 | tf_op jit(solution)/shard_map/while/body/eval_jaxpr/vmap()/reduce_sum | solution.py:37
  627.0 9.2 %subtract_reduce_fusion.2 = (f32[64,128]{1,0:T(8,128)S(1)}, f32[64,128]{1,0:T(8,128)S(1)}, f32[64,128,128]{2,1,0:T(8,128)S(1)}) fusion(f32[64,128,128]{2,1,0:T(8,128)S(1)} %multiply_reduce_fusion.11, f32[64,128]{1,0:T(8,128)S(1)} %bitcast.118, f32[64,128]{1,0:T(8,128)S(1)} %bitcast.121, f32[64,128,128]{2,1,0:T(8,128)S(1)} %fusion.71, ...), kind=kLoop, calls=%fused_computation.59.clone.1 | loop fusion | flops 38780928 | bytes 12845056 | tf_op jit(solution)/shard_map/while/body/eval_jaxpr/vmap()/reduce_sum | solution.py:37
  636.2 8.5 %multiply_reduce_fusion.12 = (f32[64,3,128]{2,1,0:T(4,128)S(1)}, f32[64,3,128]{2,1,0:T(4,128)S(1)}) fusion(f32[64,128,128]{2,1,0:T(8,128)S(1)} %get-tuple-element.363, f32[64,128,128]{2,1,0:T(8,128)S(1)} %add_sqrt_fusion.5, f32[64,3,128]{2,1,0:T(4,128)S(1)} %get-tuple-element.354, f32[64,3,128]{2,1,0:T(4,128)S(1)} %get-tuple-element.355), kind=kLoop, calls=%fused_computation.44.clone.1 | loop fusion | flops 15679488 | bytes 8781824 | tf_op jit(solution)/shard_map/while/body/eval_jaxpr/vmap()/reduce_sum | solution.py:37
  664.9 9.2 %subtract_reduce_fusion.2 = (f32[64,128]{1,0:T(8,128)S(1)}, f32[64,128]{1,0:T(8,128)S(1)}, f32[64,128,128]{2,1,0:T(8,128)S(1)}) fusion(f32[64,128,128]{2,1,0:T(8,128)S(1)} %multiply_reduce_fusion.11, f32[64,128]{1,0:T(8,128)S(1)} %bitcast.118, f32[64,128]{1,0:T(8,128)S(1)} %bitcast.121, f32[64,128,128]{2,1,0:T(8,128)S(1)} %fusion.71, ...), kind=kLoop, calls=%fused_computation.59.clone.1 | loop fusion | flops 38780928 | bytes 12845056 | tf_op jit(solution)/shard_map/while/body/eval_jaxpr/vmap()/reduce_sum | solution.py:37
  674.1 8.5 %multiply_reduce_fusion.12 = (f32[64,3,128]{2,1,0:T(4,128)S(1)}, f32[64,3,128]{2,1,0:T(4,128)S(1)}) fusion(f32[64,128,128]{2,1,0:T(8,128)S(1)} %get-tuple-element.363, f32[64,128,128]{2,1,0:T(8,128)S(1)} %add_sqrt_fusion.5, f32[64,3,128]{2,1,0:T(4,128)S(1)} %get-tuple-element.354, f32[64,3,128]{2,1,0:T(4,128)S(1)} %get-tuple-element.355), kind=kLoop, calls=%fused_computation.44.clone.1 | loop fusion | flops 15679488 | bytes 8781824 | tf_op jit(solution)/shard_map/while/body/eval_jaxpr/vmap()/reduce_sum | solution.py:37
  702.7 9.2 %subtract_reduce_fusion.2 = (f32[64,128]{1,0:T(8,128)S(1)}, f32[64,128]{1,0:T(8,128)S(1)}, f32[64,128,128]{2,1,0:T(8,128)S(1)}) fusion(f32[64,128,128]{2,1,0:T(8,128)S(1)} %multiply_reduce_fusion.11, f32[64,128]{1,0:T(8,128)S(1)} %bitcast.118, f32[64,128]{1,0:T(8,128)S(1)} %bitcast.121, f32[64,128,128]{2,1,0:T(8,128)S(1)} %fusion.71, ...), kind=kLoop, calls=%fused_computation.59.clone.1 | loop fusion | flops 38780928 | bytes 12845056 | tf_op jit(solution)/shard_map/while/body/eval_jaxpr/vmap()/reduce_sum | solution.py:37
  712.0 8.5 %multiply_reduce_fusion.12 = (f32[64,3,128]{2,1,0:T(4,128)S(1)}, f32[64,3,128]{2,1,0:T(4,128)S(1)}) fusion(f32[64,128,128]{2,1,0:T(8,128)S(1)} %get-tuple-element.363, f32[64,128,128]{2,1,0:T(8,128)S(1)} %add_sqrt_fusion.5, f32[64,3,128]{2,1,0:T(4,128)S(1)} %get-tuple-element.354, f32[64,3,128]{2,1,0:T(4,128)S(1)} %get-tuple-element.355), kind=kLoop, calls=%fused_computation.44.clone.1 | loop fusion | flops 15679488 | bytes 8781824 | tf_op jit(solution)/shard_map/while/body/eval_jaxpr/vmap()/reduce_sum | solution.py:37
  725.7 10.5 %collective-permute-done.16 = f32[192,512]{1,0:T(8,128)S(1)} collective-permute-done((f32[192,512]{1,0:T(8,128)S(1)}, f32[192,512]{1,0:T(8,128)S(1)}, u32[]{:S(2)}, u32[]{:S(2)}) %collective-permute-start.16) | collective-permute-done | bytes 393248 | tf_op jit(solution)/shard_map/ppermute | solution.py:15
  741.1 69.2 %while.27 = (s32[]{:T(128)}, f32[8,16,4,128]{3,2,1,0:T(4,128)S(1)}, f32[8,16,9,128]{3,1,0,2:T(8,128)}, s32[]{:T(128)}) while((s32[]{:T(128)}, f32[8,16,4,128]{3,2,1,0:T(4,128)S(1)}, f32[8,16,9,128]{3,1,0,2:T(8,128)}, s32[]{:T(128)}) %tuple.103), condition=%wide.region_14.15_spmd, body=%wide.region_9.14_spmd.sunk | while | flops 18925568 | bytes 11239485 | solution.py:158
  810.4 14.0 %reduce-scatter.2.cloned.1.call-done = f32[128,512]{1,0:T(8,128)} async-done(((f32[2048,512]{1,0:T(8,128)}), f32[128,512]{1,0:T(8,128)}) %reduce-scatter.2.cloned.1.call-update) | async-done | bytes 262160 | tf_op jit(solution)/shard_map/reduce_scatter | solution.py:147
  (689 shorter events, 396.0 us)
Async XLA Ops:
  6.5 84.2 %all-gather.2.cloned.1.call-start = ((), (), s32[]{:S(2)}) async-start(), calls=%async_computation.1 | async-start | bytes 10027008 | tf_op jit(solution)/shard_map/all_gather | solution.py:95
  11.9 812.5 %reduce-scatter.2.cloned.1.call-start = ((), (), s32[]{:S(2)}) async-start(), calls=%async_computation.2 | async-start | bytes 4456448 | tf_op jit(solution)/shard_map/reduce_scatter | solution.py:147
  11.9 8.5 %collective-permute-start = (s32[1,16,12]{1,0,2:T(1,128)}, s32[1,16,12]{1,0,2:T(1,128)S(1)}, u32[]{:S(2)}, u32[]{:S(2)}) collective-permute-start(s32[1,16,12]{1,0,2:T(1,128)} %param.17), channel_id=1, source_target_pairs={{0,1},{1,2},{2,3},{3,4},{4,5},{5,6},{6,7},{7,8},{8,9},{9,10},{10,1... | collective-permute-start | bytes 2312 | tf_op jit(solution)/shard_map/ppermute | solution.py:101
  14.0 6.4 collective-permute-start.8
  20.4 6.9 collective-permute-start.1
  20.4 6.9 collective-permute-start.9
  27.3 7.0 collective-permute-start.2
  27.3 7.0 collective-permute-start.10
  34.4 6.9 collective-permute-start.3
  34.4 6.9 collective-permute-start.11
  41.3 6.9 collective-permute-start.4
  41.3 7.0 collective-permute-start.12
  48.3 7.0 collective-permute-start.5
  48.3 7.0 collective-permute-start.13
  55.2 7.1 collective-permute-start.6
  55.2 7.2 collective-permute-start.14
  62.3 7.1 collective-permute-start.7
  71.3 32.1 %copy-start.4 = (s32[16,1,12]{2,0,1:T(8,128)}, s32[16,1,12]{2,0,1:T(8,128)S(1)}, u32[]{:S(2)}) copy-start(s32[16,1,12]{2,0,1:T(8,128)S(1)} %copy.34) | copy-start | bytes 2308
  103.5 9.7 %copy-start.9 = (s32[1,1024,2]{1,2,0:T(2,128)S(1)}, s32[1,1024,2]{1,2,0:T(2,128)}, u32[]{:S(2)}) copy-start(s32[1,1024,2]{1,2,0:T(2,128)} %param.18) | copy-start | bytes 24580
  111.2 4.0 collective-permute-start.15
  144.1 8.6 %copy-start.6 = (s32[16,64]{1,0:T(8,128)S(1)}, s32[16,64]{1,0:T(8,128)}, u32[]{:S(2)}) copy-start(s32[16,64]{1,0:T(8,128)} %copy-done.5) | copy-start | bytes 12292 | tf_op jit(solution)/shard_map/while
  144.1 8.6 %copy-start.8 = (s32[16,64]{1,0:T(8,128)S(1)}, s32[16,64]{1,0:T(8,128)}, u32[]{:S(2)}) copy-start(s32[16,64]{1,0:T(8,128)} %copy-done.7) | copy-start | bytes 12292 | tf_op jit(solution)/shard_map/while
  144.1 10.1 %copy-start = (f32[192,512]{1,0:T(8,128)S(1)}, f32[192,512]{1,0:T(8,128)}, u32[]{:S(2)}) copy-start(f32[192,512]{1,0:T(8,128)} %get-tuple-element.380) | copy-start | bytes 1179652 | tf_op jit(solution)/shard_map/while
  181.9 8.6 %copy-start.6 = (s32[16,64]{1,0:T(8,128)S(1)}, s32[16,64]{1,0:T(8,128)}, u32[]{:S(2)}) copy-start(s32[16,64]{1,0:T(8,128)} %copy-done.5) | copy-start | bytes 12292 | tf_op jit(solution)/shard_map/while
  182.0 8.6 %copy-start.8 = (s32[16,64]{1,0:T(8,128)S(1)}, s32[16,64]{1,0:T(8,128)}, u32[]{:S(2)}) copy-start(s32[16,64]{1,0:T(8,128)} %copy-done.7) | copy-start | bytes 12292 | tf_op jit(solution)/shard_map/while
  182.0 10.1 %copy-start = (f32[192,512]{1,0:T(8,128)S(1)}, f32[192,512]{1,0:T(8,128)}, u32[]{:S(2)}) copy-start(f32[192,512]{1,0:T(8,128)} %get-tuple-element.380) | copy-start | bytes 1179652 | tf_op jit(solution)/shard_map/while
  219.8 8.6 %copy-start.6 = (s32[16,64]{1,0:T(8,128)S(1)}, s32[16,64]{1,0:T(8,128)}, u32[]{:S(2)}) copy-start(s32[16,64]{1,0:T(8,128)} %copy-done.5) | copy-start | bytes 12292 | tf_op jit(solution)/shard_map/while
  219.8 8.6 %copy-start.8 = (s32[16,64]{1,0:T(8,128)S(1)}, s32[16,64]{1,0:T(8,128)}, u32[]{:S(2)}) copy-start(s32[16,64]{1,0:T(8,128)} %copy-done.7) | copy-start | bytes 12292 | tf_op jit(solution)/shard_map/while
  219.8 10.1 %copy-start = (f32[192,512]{1,0:T(8,128)S(1)}, f32[192,512]{1,0:T(8,128)}, u32[]{:S(2)}) copy-start(f32[192,512]{1,0:T(8,128)} %get-tuple-element.380) | copy-start | bytes 1179652 | tf_op jit(solution)/shard_map/while
  257.6 8.6 %copy-start.6 = (s32[16,64]{1,0:T(8,128)S(1)}, s32[16,64]{1,0:T(8,128)}, u32[]{:S(2)}) copy-start(s32[16,64]{1,0:T(8,128)} %copy-done.5) | copy-start | bytes 12292 | tf_op jit(solution)/shard_map/while
  257.7 8.6 %copy-start.8 = (s32[16,64]{1,0:T(8,128)S(1)}, s32[16,64]{1,0:T(8,128)}, u32[]{:S(2)}) copy-start(s32[16,64]{1,0:T(8,128)} %copy-done.7) | copy-start | bytes 12292 | tf_op jit(solution)/shard_map/while
  257.7 10.1 %copy-start = (f32[192,512]{1,0:T(8,128)S(1)}, f32[192,512]{1,0:T(8,128)}, u32[]{:S(2)}) copy-start(f32[192,512]{1,0:T(8,128)} %get-tuple-element.380) | copy-start | bytes 1179652 | tf_op jit(solution)/shard_map/while
  295.5 8.6 %copy-start.6 = (s32[16,64]{1,0:T(8,128)S(1)}, s32[16,64]{1,0:T(8,128)}, u32[]{:S(2)}) copy-start(s32[16,64]{1,0:T(8,128)} %copy-done.5) | copy-start | bytes 12292 | tf_op jit(solution)/shard_map/while
  295.5 10.1 %copy-start = (f32[192,512]{1,0:T(8,128)S(1)}, f32[192,512]{1,0:T(8,128)}, u32[]{:S(2)}) copy-start(f32[192,512]{1,0:T(8,128)} %get-tuple-element.380) | copy-start | bytes 1179652 | tf_op jit(solution)/shard_map/while
  333.4 10.1 %copy-start = (f32[192,512]{1,0:T(8,128)S(1)}, f32[192,512]{1,0:T(8,128)}, u32[]{:S(2)}) copy-start(f32[192,512]{1,0:T(8,128)} %get-tuple-element.380) | copy-start | bytes 1179652 | tf_op jit(solution)/shard_map/while
  371.2 10.1 %copy-start = (f32[192,512]{1,0:T(8,128)S(1)}, f32[192,512]{1,0:T(8,128)}, u32[]{:S(2)}) copy-start(f32[192,512]{1,0:T(8,128)} %get-tuple-element.380) | copy-start | bytes 1179652 | tf_op jit(solution)/shard_map/while
  409.1 10.1 %copy-start = (f32[192,512]{1,0:T(8,128)S(1)}, f32[192,512]{1,0:T(8,128)}, u32[]{:S(2)}) copy-start(f32[192,512]{1,0:T(8,128)} %get-tuple-element.380) | copy-start | bytes 1179652 | tf_op jit(solution)/shard_map/while
  446.9 10.1 %copy-start = (f32[192,512]{1,0:T(8,128)S(1)}, f32[192,512]{1,0:T(8,128)}, u32[]{:S(2)}) copy-start(f32[192,512]{1,0:T(8,128)} %get-tuple-element.380) | copy-start | bytes 1179652 | tf_op jit(solution)/shard_map/while
  484.8 10.1 %copy-start = (f32[192,512]{1,0:T(8,128)S(1)}, f32[192,512]{1,0:T(8,128)}, u32[]{:S(2)}) copy-start(f32[192,512]{1,0:T(8,128)} %get-tuple-element.380) | copy-start | bytes 1179652 | tf_op jit(solution)/shard_map/while
  522.6 10.1 %copy-start = (f32[192,512]{1,0:T(8,128)S(1)}, f32[192,512]{1,0:T(8,128)}, u32[]{:S(2)}) copy-start(f32[192,512]{1,0:T(8,128)} %get-tuple-element.380) | copy-start | bytes 1179652 | tf_op jit(solution)/shard_map/while
  560.5 10.1 %copy-start = (f32[192,512]{1,0:T(8,128)S(1)}, f32[192,512]{1,0:T(8,128)}, u32[]{:S(2)}) copy-start(f32[192,512]{1,0:T(8,128)} %get-tuple-element.380) | copy-start | bytes 1179652 | tf_op jit(solution)/shard_map/while
  598.4 10.1 %copy-start = (f32[192,512]{1,0:T(8,128)S(1)}, f32[192,512]{1,0:T(8,128)}, u32[]{:S(2)}) copy-start(f32[192,512]{1,0:T(8,128)} %get-tuple-element.380) | copy-start | bytes 1179652 | tf_op jit(solution)/shard_map/while
  636.2 8.6 %copy-start.6 = (s32[16,64]{1,0:T(8,128)S(1)}, s32[16,64]{1,0:T(8,128)}, u32[]{:S(2)}) copy-start(s32[16,64]{1,0:T(8,128)} %copy-done.5) | copy-start | bytes 12292 | tf_op jit(solution)/shard_map/while
  636.2 8.6 %copy-start.8 = (s32[16,64]{1,0:T(8,128)S(1)}, s32[16,64]{1,0:T(8,128)}, u32[]{:S(2)}) copy-start(s32[16,64]{1,0:T(8,128)} %copy-done.7) | copy-start | bytes 12292 | tf_op jit(solution)/shard_map/while
  636.2 10.1 %copy-start = (f32[192,512]{1,0:T(8,128)S(1)}, f32[192,512]{1,0:T(8,128)}, u32[]{:S(2)}) copy-start(f32[192,512]{1,0:T(8,128)} %get-tuple-element.380) | copy-start | bytes 1179652 | tf_op jit(solution)/shard_map/while
  674.1 10.1 %copy-start = (f32[192,512]{1,0:T(8,128)S(1)}, f32[192,512]{1,0:T(8,128)}, u32[]{:S(2)}) copy-start(f32[192,512]{1,0:T(8,128)} %get-tuple-element.380) | copy-start | bytes 1179652 | tf_op jit(solution)/shard_map/while
  711.9 10.1 %copy-start = (f32[192,512]{1,0:T(8,128)S(1)}, f32[192,512]{1,0:T(8,128)}, u32[]{:S(2)}) copy-start(f32[192,512]{1,0:T(8,128)} %get-tuple-element.380) | copy-start | bytes 1179652 | tf_op jit(solution)/shard_map/while
  723.3 12.9 %collective-permute-start.16 = (f32[192,512]{1,0:T(8,128)S(1)}, f32[192,512]{1,0:T(8,128)S(1)}, u32[]{:S(2)}, u32[]{:S(2)}) collective-permute-start(f32[192,512]{1,0:T(8,128)S(1)} %slice.109), channel_id=1, source_target_pairs={{16,0},{32,16},{48,32},{64,48},{80,64},{96,80},{112,96},{17,1},{33... | collective-permute-start | bytes 1179656 | tf_op jit(solution)/shard_map/ppermute | solution.py:15
  (86 other events, 314.4 us)
Sparse Core Ops, SparseCore 0:
  12.0 78.6 all-gather.1
  741.3 83.0 reduce-scatter.1
